TPU v7x, 512 devices: a whole 4x8x8 slice. The times are simulated.
512 devices in a mesh: depth: 16 (over z, core), freq: 32 (over x, y).
Axes of the slice: x: 4, y: 8, z: 8, core: 2. Of those that a mesh axis runs over, the one named last changes fastest.
Arguments:
- traces: bfloat16 [16384, 128], P('freq'), may hold values from -6 to 6
- shot_of_trace: int32 [32, 512], P('freq'), may hold values from 0 to 5, never falling along the last dimension, each value on 1 to 128 neighbouring positions
- receiver_cell: int32 [32, 512], P('freq'), may hold values from 0 to 511
- slot_freq: int32 [64], P('freq'), may hold values from 0 to 63, each once
- operators: bfloat16 [16, 64, 2, 512, 512], P('depth', 'freq'), may hold values from -1 to 1
- slowness: float32 [16, 512], P('depth'), may hold values from 0.5 to 2
- image_model: float32 [16, 512], P('depth'), may hold values from -3 to 3
Outputs:
- gradient: float32 [16, 512], P('depth')
- adjoint_tops: bfloat16 [16, 64, 2, 192, 512], P('depth', 'freq')
Inputs may be any that keep to these rules, and one draw needn't show every extreme that they name: `shot_of_trace`: within each row of 512 entries the numbers never fall and each of 0 to 5 appears. A program may pack these labels, and the receiver cells, several to a 32-bit word while they travel between devices. `receiver_cell`: A program may pack these labels, and the shot numbers, several to a 32-bit word while they travel between devices. `slot_freq`: each frequency number once.
All inputs are finite; a program needn't handle non-finite values.
Results may differ from a plain program's by a relative error of at most 0.023.
Values may be sent and summed in bfloat16 or wider, within the bound.
A program may use at most 192 MiB of HBM per device.

v0:
```python
import jax
import jax.numpy as jnp
from jax import lax
from jax.sharding import PartitionSpec as P

SHOTS_DEV = 6


def shifted_2(block, axis, distance):
    devices = range(lax.axis_size(axis))
    route = [(i - distance, i) for i in devices if i - distance in devices]
    return lax.ppermute(block, axis, route)


def forward_product(left_side, matrix):
    return jnp.einsum("fsx,fyx->fsy", left_side, matrix, preferred_element_type=jnp.float32)


def adjoint_product(left_side, matrix):
    return jnp.einsum("fsy,fyx->fsx", left_side, matrix, preferred_element_type=jnp.float32)


def descend(wavefield, matrices, cosines, sine_values):
    cos_here = cosines[0][:, None, :]
    sin_here = sine_values[0][:, None, :]
    real_part = cos_here * wavefield[:, 0] - sin_here * wavefield[:, 1]
    imag_part = cos_here * wavefield[:, 1] + sin_here * wavefield[:, 0]
    shifted = jnp.stack([real_part, imag_part], axis=1).astype(jnp.bfloat16)
    shifted_list = [shifted]
    mat_real = matrices[0, :, 0]
    mat_imag = matrices[0, :, 1]
    new_real = forward_product(shifted[:, 0], mat_real) - forward_product(shifted[:, 1], mat_imag)
    new_imag = forward_product(shifted[:, 0], mat_imag) + forward_product(shifted[:, 1], mat_real)
    wavefield = jnp.stack([new_real, new_imag], axis=1)
    return (wavefield, jnp.stack(shifted_list))


def ascend(adjoint, matrices, cosines, sine_values, shifted_all, model_rows):
    level_count = matrices.shape[0]
    image_terms = [None] * level_count
    for level_index in reversed(range(level_count)):
        cos_here = cosines[level_index][:, None, :]
        sin_here = sine_values[level_index][:, None, :]
        shifted = shifted_all[level_index].astype(jnp.float32)
        source = adjoint + model_rows[level_index] * shifted
        image_terms[level_index] = jnp.sum(
            shifted[:, 0] * source[:, 0] + shifted[:, 1] * source[:, 1], axis=(0, 1)
        )
        rounded = source.astype(jnp.bfloat16)
        mat_real = matrices[level_index, :, 0]
        mat_imag = matrices[level_index, :, 1]
        back_real = adjoint_product(rounded[:, 0], mat_real) + adjoint_product(
            rounded[:, 1], mat_imag
        )
        back_imag = adjoint_product(rounded[:, 1], mat_real) - adjoint_product(
            rounded[:, 0], mat_imag
        )
        adjoint = jnp.stack(
            [
                cos_here * back_real + sin_here * back_imag,
                cos_here * back_imag - sin_here * back_real,
            ],
            axis=1,
        )
    return (adjoint, jnp.stack(image_terms))


def body(traces, shot_of_trace, receiver_cell, slot_freq, operators, slowness, image_model):
    groups = lax.axis_size("freq")
    sections = lax.axis_size("depth")
    section = lax.axis_index("depth")
    level_count = operators.shape[0]
    local_freqs = operators.shape[1]
    lateral = operators.shape[-1]
    shot_total = SHOTS_DEV * groups
    columns = traces.T
    arrived = lax.all_to_all(columns, "freq", split_axis=0, concat_axis=1, tiled=True)
    shot_labels, cell_labels = (
        lax.all_gather(shot_of_trace, "freq", axis=0, tiled=True),
        lax.all_gather(receiver_cell, "freq", axis=0, tiled=True),
    )
    block_base = (jnp.arange(groups, dtype=jnp.int32) * SHOTS_DEV)[:, None]
    flat_index = ((shot_labels + block_base) * lateral + cell_labels).reshape(-1)
    summed = jax.ops.segment_sum(
        arrived.T.astype(jnp.float32), flat_index, num_segments=shot_total * lateral
    )
    surface = summed.T.astype(jnp.bfloat16)
    surface = surface.reshape(local_freqs, 2, shot_total, lateral)
    angle_scale = 0.1 * (slot_freq.astype(jnp.float32) + 1.0)
    phase_angle = angle_scale[None, :, None] * slowness[:, None, :]
    cosines = jnp.cos(phase_angle)
    sine_values = jnp.sin(phase_angle)
    freq_parts, shot_parts = (local_freqs, 1)
    unit_count = freq_parts * shot_parts
    freq_width = local_freqs // freq_parts
    shot_width = shot_total // shot_parts
    turn_count = sections + unit_count - 1
    block_shape = (freq_width, 2, shot_width, lateral)

    def locate(offset):
        active = (offset >= 0) & (offset < unit_count)
        clipped = jnp.clip(offset, 0, unit_count - 1)
        return (active, clipped // shot_parts * freq_width, clipped % shot_parts * shot_width)

    def slot_tables(freq_start):
        matrices = lax.dynamic_slice_in_dim(operators, freq_start, freq_width, 1)
        cos_block = lax.dynamic_slice_in_dim(cosines, freq_start, freq_width, 1)
        sin_block = lax.dynamic_slice_in_dim(sine_values, freq_start, freq_width, 1)
        return (matrices, cos_block, sin_block)

    def down_turn(turn_index, loop_state):
        incoming, stored = loop_state
        active, freq_start, shot_start = locate(turn_index - section)
        top_block = lax.dynamic_slice(surface, (freq_start, 0, shot_start, 0), block_shape)
        entering = jnp.where(section == 0, top_block, incoming).astype(jnp.float32)

        def down_working(stored_now):
            matrices, cos_block, sin_block = slot_tables(freq_start)
            leaving, shifted_all = descend(entering, matrices, cos_block, sin_block)
            stored_now = lax.dynamic_update_slice(
                stored_now, shifted_all, (0, freq_start, 0, shot_start, 0)
            )
            return (leaving.astype(jnp.bfloat16), stored_now)

        def down_passing(stored_now):
            return (jnp.zeros(block_shape, jnp.bfloat16), stored_now)

        leaving, stored = lax.cond(active, down_working, down_passing, stored)
        incoming = shifted_2(leaving, "depth", 1)
        return (incoming, stored)

    stored_start = jnp.zeros((level_count, local_freqs, 2, shot_total, lateral), jnp.bfloat16)
    ignored, stored = lax.fori_loop(
        0, turn_count, down_turn, (jnp.zeros(block_shape, jnp.bfloat16), stored_start)
    )

    def up_turn(turn_index, loop_state):
        incoming, top_fields, image_terms = loop_state
        active, freq_start, shot_start = locate(turn_index - (sections - 1 - section))
        entering = jnp.where(section == sections - 1, jnp.zeros_like(incoming), incoming).astype(
            jnp.float32
        )

        def up_working(carried):
            fields_now, terms_now = carried
            matrices, cos_block, sin_block = slot_tables(freq_start)
            shifted_all = lax.dynamic_slice(
                stored, (0, freq_start, 0, shot_start, 0), (level_count,) + block_shape
            )
            adjoint, terms = ascend(
                entering, matrices, cos_block, sin_block, shifted_all, image_model
            )
            leaving = adjoint.astype(jnp.bfloat16)
            fields_now = lax.dynamic_update_slice(
                fields_now, leaving, (freq_start, 0, shot_start, 0)
            )
            return (leaving, (fields_now, terms_now + terms))

        def up_passing(carried):
            return (jnp.zeros(block_shape, jnp.bfloat16), carried)

        leaving, (top_fields, image_terms) = lax.cond(
            active, up_working, up_passing, (top_fields, image_terms)
        )
        incoming = shifted_2(leaving, "depth", -1)
        return (incoming, top_fields, image_terms)

    fields_start = jnp.zeros((local_freqs, 2, shot_total, lateral), jnp.bfloat16)
    terms_start = jnp.zeros((level_count, lateral), jnp.float32)
    ignored, top_fields, image_terms = lax.fori_loop(
        0, turn_count, up_turn, (jnp.zeros(block_shape, jnp.bfloat16), fields_start, terms_start)
    )
    total_terms = lax.psum(image_terms, "freq")
    gradient = total_terms / (local_freqs * groups * shot_total)
    return (gradient, top_fields[None])


def solution(mesh):
    in_specs = (
        P("freq", None),
        P("freq", None),
        P("freq", None),
        P("freq"),
        P("depth", "freq", None, None, None),
        P("depth", None),
        P("depth", None),
    )
    out_specs = (P("depth", None), P("depth", "freq", None, None, None))
    return jax.shard_map(body, mesh=mesh, in_specs=in_specs, out_specs=out_specs, check_vma=False)
```

profile of v0, /device:TPU:1, one launch (start us, length us, event | category | flops | bytes accessed | tf_op | source)
XLA Modules:
  0.0 757.4 jit_solution(16451523161739914142)
XLA Ops:
  2.3 10.5 %all-to-all-start = ((bf16[32,4,512]{2,1,0:T(4,128)(2,1)}), bf16[32,4,512]{2,1,0:T(4,128)(2,1)S(1)}, u32[]{:S(2)}, u32[]{:S(2)}) async-start(bf16[32,4,512]{2,1,0:T(4,128)(2,1)} %all_to_all.10), calls=%async_computation | async-start | bytes 262144 | tf_op jit(solution)/shard_map/all_to_all | solution.py:77
  12.9 37.4 %all-gather = s32[32,1,512]{2,1,0:T(1,128)S(1)} all-gather(s32[1,1,512]{2,1,0:T(1,128)} %bitcast.103), channel_id=1, replica_groups=mesh['depth'=16,'freq'=32] {'freq'}, dimensions={0}, use_global_device_ids=true | all-gather | bytes 67584 | tf_op jit(solution)/shard_map/all_gather | solution.py:79
  50.2 35.1 %all-gather.1 = s32[32,1,512]{2,1,0:T(1,128)S(1)} all-gather(s32[1,1,512]{2,1,0:T(1,128)} %bitcast.104), channel_id=1, replica_groups=mesh['depth'=16,'freq'=32] {'freq'}, dimensions={0}, use_global_device_ids=true | all-gather | bytes 67584 | tf_op jit(solution)/shard_map/all_gather | solution.py:80
  86.1 5.0 copy.17
  91.1 107.4 %scatter_custom_fusion = f32[98304,4]{1,0:T(8,128)} fusion(s32[16384]{0:T(1024)S(1)} %bitcast.101, f32[16384,4]{1,0:T(8,128)} %copy.17, f32[]{:T(128)} %constant.196.clone.1), kind=kCustom, calls=%fused_computation.60 | custom fusion | flops 65536 | bytes 1573376 | tf_op jit(solution)/shard_map/scatter-add | solution.py:84
  198.5 25.4 %convert_bitcast_fusion = bf16[4,98304]{0,1:T(8,128)(2,1)} fusion(f32[98304,4]{1,0:T(8,128)} %scatter_custom_fusion), kind=kLoop, calls=%fused_computation.59 | loop fusion | flops 393216 | bytes 2359296 | tf_op jit(solution)/shard_map/convert_element_type | solution.py:87
  223.9 18.5 %copy.18 = bf16[4,98304]{1,0:T(4,128)(2,1)S(1)} copy(bf16[4,98304]{0,1:T(8,128)(2,1)} %convert_bitcast_fusion) | data formatting | bytes 1572864 | tf_op jit(solution)/shard_map/convert_element_type | solution.py:87
  244.4 220.4 %while.43 = (s32[]{:T(128)}, bf16[1,2,192,512]{3,2,1,0:T(8,128)(2,1)S(1)}, bf16[1,2,2,192,512]{4,3,2,1,0:T(8,128)(2,1)}, s32[]{:T(128)}, pred[]{:T(512)}, /*inde...) while((s32[]{:T(128)}, ...), condition=%wide.region_4.5_spmd.clone.clone, body=%wide.region_1.4_spmd.clone.clone.sunk | while | flops 405210112 | bytes 10766710 | solution.py:133
  246.4 29.2 %collective-permute-start = (bf16[1,2,192,512]{3,2,1,0:T(8,128)(2,1)}, bf16[1,2,192,512]{3,2,1,0:T(8,128)(2,1)S(1)}, u32[]{:S(2)}, u32[]{:S(2)}) collective-permute-start(bf16[1,2,192,512]{3,2,1,0:T(8,128)(2,1)} %get-tuple-element.934), channel_id=1, source_target_pairs={{0,32},{32,64},{64,96},{96,128},{128,160},{160,192},{192,224},{224... | collective-permute-start | bytes 1179656 | tf_op jit(solution)/shard_map/while/body/eval_jaxpr/ppermute | solution.py:12
  275.5 5.0 collective-permute-done
  307.3 6.7 collective-permute-start
  465.8 233.0 %while.44 = (s32[]{:T(128)}, bf16[1,2,192,512]{3,2,1,0:T(8,128)(2,1)S(1)}, bf16[2,2,192,512]{3,2,1,0:T(8,128)(2,1)}, f32[1,512]{1,0:T(1,128)S(1)}, s32[]{:T(128)...) while((s32[]{:T(128)}, ...), condition=%wide.region_9.10_spmd.clone.clone, body=%wide.region_5.9_spmd.clone.clone.sunk | while | flops 406193152 | bytes 24146412 | solution.py:170
  468.6 8.0 %collective-permute-done.1 = bf16[1,2,192,512]{3,2,1,0:T(8,128)(2,1)S(1)} collective-permute-done((bf16[1,2,192,512]{3,2,1,0:T(8,128)(2,1)}, bf16[1,2,192,512]{3,2,1,0:T(8,128)(2,1)S(1)}, u32[]{:S(2)}, u32[]{:S(2)}) %collective-permute-start.1) | collective-permute-done | bytes 393248 | tf_op jit(solution)/shard_map/while/body/eval_jaxpr/ppermute | solution.py:12
  479.5 7.4 collective-permute-done.1
  489.7 7.6 %collective-permute-done.1 = bf16[1,2,192,512]{3,2,1,0:T(8,128)(2,1)S(1)} collective-permute-done((bf16[1,2,192,512]{3,2,1,0:T(8,128)(2,1)}, bf16[1,2,192,512]{3,2,1,0:T(8,128)(2,1)S(1)}, u32[]{:S(2)}, u32[]{:S(2)}) %collective-permute-start.1) | collective-permute-done | bytes 393248 | tf_op jit(solution)/shard_map/while/body/eval_jaxpr/ppermute | solution.py:12
  500.2 8.5 %collective-permute-done.1 = bf16[1,2,192,512]{3,2,1,0:T(8,128)(2,1)S(1)} collective-permute-done((bf16[1,2,192,512]{3,2,1,0:T(8,128)(2,1)}, bf16[1,2,192,512]{3,2,1,0:T(8,128)(2,1)S(1)}, u32[]{:S(2)}, u32[]{:S(2)}) %collective-permute-start.1) | collective-permute-done | bytes 393248 | tf_op jit(solution)/shard_map/while/body/eval_jaxpr/ppermute | solution.py:12
  511.5 9.2 %collective-permute-done.1 = bf16[1,2,192,512]{3,2,1,0:T(8,128)(2,1)S(1)} collective-permute-done((bf16[1,2,192,512]{3,2,1,0:T(8,128)(2,1)}, bf16[1,2,192,512]{3,2,1,0:T(8,128)(2,1)S(1)}, u32[]{:S(2)}, u32[]{:S(2)}) %collective-permute-start.1) | collective-permute-done | bytes 393248 | tf_op jit(solution)/shard_map/while/body/eval_jaxpr/ppermute | solution.py:12
  523.5 8.5 %collective-permute-done.1 = bf16[1,2,192,512]{3,2,1,0:T(8,128)(2,1)S(1)} collective-permute-done((bf16[1,2,192,512]{3,2,1,0:T(8,128)(2,1)}, bf16[1,2,192,512]{3,2,1,0:T(8,128)(2,1)S(1)}, u32[]{:S(2)}, u32[]{:S(2)}) %collective-permute-start.1) | collective-permute-done | bytes 393248 | tf_op jit(solution)/shard_map/while/body/eval_jaxpr/ppermute | solution.py:12
  534.8 9.2 %collective-permute-done.1 = bf16[1,2,192,512]{3,2,1,0:T(8,128)(2,1)S(1)} collective-permute-done((bf16[1,2,192,512]{3,2,1,0:T(8,128)(2,1)}, bf16[1,2,192,512]{3,2,1,0:T(8,128)(2,1)S(1)}, u32[]{:S(2)}, u32[]{:S(2)}) %collective-permute-start.1) | collective-permute-done | bytes 393248 | tf_op jit(solution)/shard_map/while/body/eval_jaxpr/ppermute | solution.py:12
  546.9 8.6 %collective-permute-done.1 = bf16[1,2,192,512]{3,2,1,0:T(8,128)(2,1)S(1)} collective-permute-done((bf16[1,2,192,512]{3,2,1,0:T(8,128)(2,1)}, bf16[1,2,192,512]{3,2,1,0:T(8,128)(2,1)S(1)}, u32[]{:S(2)}, u32[]{:S(2)}) %collective-permute-start.1) | collective-permute-done | bytes 393248 | tf_op jit(solution)/shard_map/while/body/eval_jaxpr/ppermute | solution.py:12
  558.3 8.6 %collective-permute-done.1 = bf16[1,2,192,512]{3,2,1,0:T(8,128)(2,1)S(1)} collective-permute-done((bf16[1,2,192,512]{3,2,1,0:T(8,128)(2,1)}, bf16[1,2,192,512]{3,2,1,0:T(8,128)(2,1)S(1)}, u32[]{:S(2)}, u32[]{:S(2)}) %collective-permute-start.1) | collective-permute-done | bytes 393248 | tf_op jit(solution)/shard_map/while/body/eval_jaxpr/ppermute | solution.py:12
  569.8 8.6 %collective-permute-done.1 = bf16[1,2,192,512]{3,2,1,0:T(8,128)(2,1)S(1)} collective-permute-done((bf16[1,2,192,512]{3,2,1,0:T(8,128)(2,1)}, bf16[1,2,192,512]{3,2,1,0:T(8,128)(2,1)S(1)}, u32[]{:S(2)}, u32[]{:S(2)}) %collective-permute-start.1) | collective-permute-done | bytes 393248 | tf_op jit(solution)/shard_map/while/body/eval_jaxpr/ppermute | solution.py:12
  581.2 8.6 %collective-permute-done.1 = bf16[1,2,192,512]{3,2,1,0:T(8,128)(2,1)S(1)} collective-permute-done((bf16[1,2,192,512]{3,2,1,0:T(8,128)(2,1)}, bf16[1,2,192,512]{3,2,1,0:T(8,128)(2,1)S(1)}, u32[]{:S(2)}, u32[]{:S(2)}) %collective-permute-start.1) | collective-permute-done | bytes 393248 | tf_op jit(solution)/shard_map/while/body/eval_jaxpr/ppermute | solution.py:12
  592.6 8.6 %collective-permute-done.1 = bf16[1,2,192,512]{3,2,1,0:T(8,128)(2,1)S(1)} collective-permute-done((bf16[1,2,192,512]{3,2,1,0:T(8,128)(2,1)}, bf16[1,2,192,512]{3,2,1,0:T(8,128)(2,1)S(1)}, u32[]{:S(2)}, u32[]{:S(2)}) %collective-permute-start.1) | collective-permute-done | bytes 393248 | tf_op jit(solution)/shard_map/while/body/eval_jaxpr/ppermute | solution.py:12
  604.0 8.6 %collective-permute-done.1 = bf16[1,2,192,512]{3,2,1,0:T(8,128)(2,1)S(1)} collective-permute-done((bf16[1,2,192,512]{3,2,1,0:T(8,128)(2,1)}, bf16[1,2,192,512]{3,2,1,0:T(8,128)(2,1)S(1)}, u32[]{:S(2)}, u32[]{:S(2)}) %collective-permute-start.1) | collective-permute-done | bytes 393248 | tf_op jit(solution)/shard_map/while/body/eval_jaxpr/ppermute | solution.py:12
  615.5 41.2 %collective-permute-done.1 = bf16[1,2,192,512]{3,2,1,0:T(8,128)(2,1)S(1)} collective-permute-done((bf16[1,2,192,512]{3,2,1,0:T(8,128)(2,1)}, bf16[1,2,192,512]{3,2,1,0:T(8,128)(2,1)S(1)}, u32[]{:S(2)}, u32[]{:S(2)}) %collective-permute-start.1) | collective-permute-done | bytes 393248 | tf_op jit(solution)/shard_map/while/body/eval_jaxpr/ppermute | solution.py:12
  656.8 5.9 conditional.9
  664.6 8.6 %collective-permute-done.1 = bf16[1,2,192,512]{3,2,1,0:T(8,128)(2,1)S(1)} collective-permute-done((bf16[1,2,192,512]{3,2,1,0:T(8,128)(2,1)}, bf16[1,2,192,512]{3,2,1,0:T(8,128)(2,1)S(1)}, u32[]{:S(2)}, u32[]{:S(2)}) %collective-permute-start.1) | collective-permute-done | bytes 393248 | tf_op jit(solution)/shard_map/while/body/eval_jaxpr/ppermute | solution.py:12
  673.4 5.9 conditional.9
  681.2 7.4 collective-permute-done.1
  691.4 7.4 collective-permute-done.1
  698.8 58.1 %psum.7 = f32[1,512]{1,0:T(1,128)S(1)} all-reduce(f32[1,512]{1,0:T(1,128)S(1)} %get-tuple-element.625), channel_id=1, replica_groups=mesh['depth'=16,'freq'=32] {'freq'}, use_global_device_ids=true, to_apply=%region_10.11 | all-reduce | flops 512 | bytes 4096 | tf_op jit(solution)/shard_map/psum | solution.py:173
  (247 shorter events, 272.9 us)
Async XLA Ops:
  2.3 83.7 %all-to-all-start = ((bf16[32,4,512]{2,1,0:T(4,128)(2,1)}), bf16[32,4,512]{2,1,0:T(4,128)(2,1)S(1)}, u32[]{:S(2)}, u32[]{:S(2)}) async-start(bf16[32,4,512]{2,1,0:T(4,128)(2,1)} %all_to_all.10), calls=%async_computation | async-start | bytes 262144 | tf_op jit(solution)/shard_map/all_to_all | solution.py:77
  246.4 34.2 %collective-permute-start = (bf16[1,2,192,512]{3,2,1,0:T(8,128)(2,1)}, bf16[1,2,192,512]{3,2,1,0:T(8,128)(2,1)S(1)}, u32[]{:S(2)}, u32[]{:S(2)}) collective-permute-start(bf16[1,2,192,512]{3,2,1,0:T(8,128)(2,1)} %get-tuple-element.934), channel_id=1, source_target_pairs={{0,32},{32,64},{64,96},{96,128},{128,160},{160,192},{192,224},{224... | collective-permute-start | bytes 1179656 | tf_op jit(solution)/shard_map/while/body/eval_jaxpr/ppermute | solution.py:12
  307.3 11.7 %collective-permute-start = (bf16[1,2,192,512]{3,2,1,0:T(8,128)(2,1)}, bf16[1,2,192,512]{3,2,1,0:T(8,128)(2,1)S(1)}, u32[]{:S(2)}, u32[]{:S(2)}) collective-permute-start(bf16[1,2,192,512]{3,2,1,0:T(8,128)(2,1)} %get-tuple-element.934), channel_id=1, source_target_pairs={{0,32},{32,64},{64,96},{96,128},{128,160},{160,192},{192,224},{224... | collective-permute-start | bytes 1179656 | tf_op jit(solution)/shard_map/while/body/eval_jaxpr/ppermute | solution.py:12
  320.9 9.3 %collective-permute-start = (bf16[1,2,192,512]{3,2,1,0:T(8,128)(2,1)}, bf16[1,2,192,512]{3,2,1,0:T(8,128)(2,1)S(1)}, u32[]{:S(2)}, u32[]{:S(2)}) collective-permute-start(bf16[1,2,192,512]{3,2,1,0:T(8,128)(2,1)} %get-tuple-element.934), channel_id=1, source_target_pairs={{0,32},{32,64},{64,96},{96,128},{128,160},{160,192},{192,224},{224... | collective-permute-start | bytes 1179656 | tf_op jit(solution)/shard_map/while/body/eval_jaxpr/ppermute | solution.py:12
  332.1 9.3 %collective-permute-start = (bf16[1,2,192,512]{3,2,1,0:T(8,128)(2,1)}, bf16[1,2,192,512]{3,2,1,0:T(8,128)(2,1)S(1)}, u32[]{:S(2)}, u32[]{:S(2)}) collective-permute-start(bf16[1,2,192,512]{3,2,1,0:T(8,128)(2,1)} %get-tuple-element.934), channel_id=1, source_target_pairs={{0,32},{32,64},{64,96},{96,128},{128,160},{160,192},{192,224},{224... | collective-permute-start | bytes 1179656 | tf_op jit(solution)/shard_map/while/body/eval_jaxpr/ppermute | solution.py:12
  343.3 9.3 %collective-permute-start = (bf16[1,2,192,512]{3,2,1,0:T(8,128)(2,1)}, bf16[1,2,192,512]{3,2,1,0:T(8,128)(2,1)S(1)}, u32[]{:S(2)}, u32[]{:S(2)}) collective-permute-start(bf16[1,2,192,512]{3,2,1,0:T(8,128)(2,1)} %get-tuple-element.934), channel_id=1, source_target_pairs={{0,32},{32,64},{64,96},{96,128},{128,160},{160,192},{192,224},{224... | collective-permute-start | bytes 1179656 | tf_op jit(solution)/shard_map/while/body/eval_jaxpr/ppermute | solution.py:12
  354.6 9.3 %collective-permute-start = (bf16[1,2,192,512]{3,2,1,0:T(8,128)(2,1)}, bf16[1,2,192,512]{3,2,1,0:T(8,128)(2,1)S(1)}, u32[]{:S(2)}, u32[]{:S(2)}) collective-permute-start(bf16[1,2,192,512]{3,2,1,0:T(8,128)(2,1)} %get-tuple-element.934), channel_id=1, source_target_pairs={{0,32},{32,64},{64,96},{96,128},{128,160},{160,192},{192,224},{224... | collective-permute-start | bytes 1179656 | tf_op jit(solution)/shard_map/while/body/eval_jaxpr/ppermute | solution.py:12
  365.8 9.3 %collective-permute-start = (bf16[1,2,192,512]{3,2,1,0:T(8,128)(2,1)}, bf16[1,2,192,512]{3,2,1,0:T(8,128)(2,1)S(1)}, u32[]{:S(2)}, u32[]{:S(2)}) collective-permute-start(bf16[1,2,192,512]{3,2,1,0:T(8,128)(2,1)} %get-tuple-element.934), channel_id=1, source_target_pairs={{0,32},{32,64},{64,96},{96,128},{128,160},{160,192},{192,224},{224... | collective-permute-start | bytes 1179656 | tf_op jit(solution)/shard_map/while/body/eval_jaxpr/ppermute | solution.py:12
  377.0 9.3 %collective-permute-start = (bf16[1,2,192,512]{3,2,1,0:T(8,128)(2,1)}, bf16[1,2,192,512]{3,2,1,0:T(8,128)(2,1)S(1)}, u32[]{:S(2)}, u32[]{:S(2)}) collective-permute-start(bf16[1,2,192,512]{3,2,1,0:T(8,128)(2,1)} %get-tuple-element.934), channel_id=1, source_target_pairs={{0,32},{32,64},{64,96},{96,128},{128,160},{160,192},{192,224},{224... | collective-permute-start | bytes 1179656 | tf_op jit(solution)/shard_map/while/body/eval_jaxpr/ppermute | solution.py:12
  388.2 9.3 %collective-permute-start = (bf16[1,2,192,512]{3,2,1,0:T(8,128)(2,1)}, bf16[1,2,192,512]{3,2,1,0:T(8,128)(2,1)S(1)}, u32[]{:S(2)}, u32[]{:S(2)}) collective-permute-start(bf16[1,2,192,512]{3,2,1,0:T(8,128)(2,1)} %get-tuple-element.934), channel_id=1, source_target_pairs={{0,32},{32,64},{64,96},{96,128},{128,160},{160,192},{192,224},{224... | collective-permute-start | bytes 1179656 | tf_op jit(solution)/shard_map/while/body/eval_jaxpr/ppermute | solution.py:12
  399.4 9.3 %collective-permute-start = (bf16[1,2,192,512]{3,2,1,0:T(8,128)(2,1)}, bf16[1,2,192,512]{3,2,1,0:T(8,128)(2,1)S(1)}, u32[]{:S(2)}, u32[]{:S(2)}) collective-permute-start(bf16[1,2,192,512]{3,2,1,0:T(8,128)(2,1)} %get-tuple-element.934), channel_id=1, source_target_pairs={{0,32},{32,64},{64,96},{96,128},{128,160},{160,192},{192,224},{224... | collective-permute-start | bytes 1179656 | tf_op jit(solution)/shard_map/while/body/eval_jaxpr/ppermute | solution.py:12
  410.6 9.3 %collective-permute-start = (bf16[1,2,192,512]{3,2,1,0:T(8,128)(2,1)}, bf16[1,2,192,512]{3,2,1,0:T(8,128)(2,1)S(1)}, u32[]{:S(2)}, u32[]{:S(2)}) collective-permute-start(bf16[1,2,192,512]{3,2,1,0:T(8,128)(2,1)} %get-tuple-element.934), channel_id=1, source_target_pairs={{0,32},{32,64},{64,96},{96,128},{128,160},{160,192},{192,224},{224... | collective-permute-start | bytes 1179656 | tf_op jit(solution)/shard_map/while/body/eval_jaxpr/ppermute | solution.py:12
  421.8 9.3 %collective-permute-start = (bf16[1,2,192,512]{3,2,1,0:T(8,128)(2,1)}, bf16[1,2,192,512]{3,2,1,0:T(8,128)(2,1)S(1)}, u32[]{:S(2)}, u32[]{:S(2)}) collective-permute-start(bf16[1,2,192,512]{3,2,1,0:T(8,128)(2,1)} %get-tuple-element.934), channel_id=1, source_target_pairs={{0,32},{32,64},{64,96},{96,128},{128,160},{160,192},{192,224},{224... | collective-permute-start | bytes 1179656 | tf_op jit(solution)/shard_map/while/body/eval_jaxpr/ppermute | solution.py:12
  433.1 9.3 %collective-permute-start = (bf16[1,2,192,512]{3,2,1,0:T(8,128)(2,1)}, bf16[1,2,192,512]{3,2,1,0:T(8,128)(2,1)S(1)}, u32[]{:S(2)}, u32[]{:S(2)}) collective-permute-start(bf16[1,2,192,512]{3,2,1,0:T(8,128)(2,1)} %get-tuple-element.934), channel_id=1, source_target_pairs={{0,32},{32,64},{64,96},{96,128},{128,160},{160,192},{192,224},{224... | collective-permute-start | bytes 1179656 | tf_op jit(solution)/shard_map/while/body/eval_jaxpr/ppermute | solution.py:12
  444.3 9.3 %collective-permute-start = (bf16[1,2,192,512]{3,2,1,0:T(8,128)(2,1)}, bf16[1,2,192,512]{3,2,1,0:T(8,128)(2,1)S(1)}, u32[]{:S(2)}, u32[]{:S(2)}) collective-permute-start(bf16[1,2,192,512]{3,2,1,0:T(8,128)(2,1)} %get-tuple-element.934), channel_id=1, source_target_pairs={{0,32},{32,64},{64,96},{96,128},{128,160},{160,192},{192,224},{224... | collective-permute-start | bytes 1179656 | tf_op jit(solution)/shard_map/while/body/eval_jaxpr/ppermute | solution.py:12
  455.5 9.3 %collective-permute-start = (bf16[1,2,192,512]{3,2,1,0:T(8,128)(2,1)}, bf16[1,2,192,512]{3,2,1,0:T(8,128)(2,1)S(1)}, u32[]{:S(2)}, u32[]{:S(2)}) collective-permute-start(bf16[1,2,192,512]{3,2,1,0:T(8,128)(2,1)} %get-tuple-element.934), channel_id=1, source_target_pairs={{0,32},{32,64},{64,96},{96,128},{128,160},{160,192},{192,224},{224... | collective-permute-start | bytes 1179656 | tf_op jit(solution)/shard_map/while/body/eval_jaxpr/ppermute | solution.py:12
  466.7 9.9 %collective-permute-start.1 = (bf16[1,2,192,512]{3,2,1,0:T(8,128)(2,1)}, bf16[1,2,192,512]{3,2,1,0:T(8,128)(2,1)S(1)}, u32[]{:S(2)}, u32[]{:S(2)}) collective-permute-start(bf16[1,2,192,512]{3,2,1,0:T(8,128)(2,1)} %get-tuple-element.947), channel_id=1, source_target_pairs={{32,0},{64,32},{96,64},{128,96},{160,128},{192,160},{224,192},{256... | collective-permute-start | bytes 1179656 | tf_op jit(solution)/shard_map/while/body/eval_jaxpr/ppermute | solution.py:12
  487.8 9.5 %collective-permute-start.1 = (bf16[1,2,192,512]{3,2,1,0:T(8,128)(2,1)}, bf16[1,2,192,512]{3,2,1,0:T(8,128)(2,1)S(1)}, u32[]{:S(2)}, u32[]{:S(2)}) collective-permute-start(bf16[1,2,192,512]{3,2,1,0:T(8,128)(2,1)} %get-tuple-element.947), channel_id=1, source_target_pairs={{32,0},{64,32},{96,64},{128,96},{160,128},{192,160},{224,192},{256... | collective-permute-start | bytes 1179656 | tf_op jit(solution)/shard_map/while/body/eval_jaxpr/ppermute | solution.py:12
  498.2 10.4 %collective-permute-start.1 = (bf16[1,2,192,512]{3,2,1,0:T(8,128)(2,1)}, bf16[1,2,192,512]{3,2,1,0:T(8,128)(2,1)S(1)}, u32[]{:S(2)}, u32[]{:S(2)}) collective-permute-start(bf16[1,2,192,512]{3,2,1,0:T(8,128)(2,1)} %get-tuple-element.947), channel_id=1, source_target_pairs={{32,0},{64,32},{96,64},{128,96},{160,128},{192,160},{224,192},{256... | collective-permute-start | bytes 1179656 | tf_op jit(solution)/shard_map/while/body/eval_jaxpr/ppermute | solution.py:12
  509.5 11.1 %collective-permute-start.1 = (bf16[1,2,192,512]{3,2,1,0:T(8,128)(2,1)}, bf16[1,2,192,512]{3,2,1,0:T(8,128)(2,1)S(1)}, u32[]{:S(2)}, u32[]{:S(2)}) collective-permute-start(bf16[1,2,192,512]{3,2,1,0:T(8,128)(2,1)} %get-tuple-element.947), channel_id=1, source_target_pairs={{32,0},{64,32},{96,64},{128,96},{160,128},{192,160},{224,192},{256... | collective-permute-start | bytes 1179656 | tf_op jit(solution)/shard_map/while/body/eval_jaxpr/ppermute | solution.py:12
  521.6 10.4 %collective-permute-start.1 = (bf16[1,2,192,512]{3,2,1,0:T(8,128)(2,1)}, bf16[1,2,192,512]{3,2,1,0:T(8,128)(2,1)S(1)}, u32[]{:S(2)}, u32[]{:S(2)}) collective-permute-start(bf16[1,2,192,512]{3,2,1,0:T(8,128)(2,1)} %get-tuple-element.947), channel_id=1, source_target_pairs={{32,0},{64,32},{96,64},{128,96},{160,128},{192,160},{224,192},{256... | collective-permute-start | bytes 1179656 | tf_op jit(solution)/shard_map/while/body/eval_jaxpr/ppermute | solution.py:12
  532.9 11.1 %collective-permute-start.1 = (bf16[1,2,192,512]{3,2,1,0:T(8,128)(2,1)}, bf16[1,2,192,512]{3,2,1,0:T(8,128)(2,1)S(1)}, u32[]{:S(2)}, u32[]{:S(2)}) collective-permute-start(bf16[1,2,192,512]{3,2,1,0:T(8,128)(2,1)} %get-tuple-element.947), channel_id=1, source_target_pairs={{32,0},{64,32},{96,64},{128,96},{160,128},{192,160},{224,192},{256... | collective-permute-start | bytes 1179656 | tf_op jit(solution)/shard_map/while/body/eval_jaxpr/ppermute | solution.py:12
  545.0 10.5 %collective-permute-start.1 = (bf16[1,2,192,512]{3,2,1,0:T(8,128)(2,1)}, bf16[1,2,192,512]{3,2,1,0:T(8,128)(2,1)S(1)}, u32[]{:S(2)}, u32[]{:S(2)}) collective-permute-start(bf16[1,2,192,512]{3,2,1,0:T(8,128)(2,1)} %get-tuple-element.947), channel_id=1, source_target_pairs={{32,0},{64,32},{96,64},{128,96},{160,128},{192,160},{224,192},{256... | collective-permute-start | bytes 1179656 | tf_op jit(solution)/shard_map/while/body/eval_jaxpr/ppermute | solution.py:12
  556.4 10.5 %collective-permute-start.1 = (bf16[1,2,192,512]{3,2,1,0:T(8,128)(2,1)}, bf16[1,2,192,512]{3,2,1,0:T(8,128)(2,1)S(1)}, u32[]{:S(2)}, u32[]{:S(2)}) collective-permute-start(bf16[1,2,192,512]{3,2,1,0:T(8,128)(2,1)} %get-tuple-element.947), channel_id=1, source_target_pairs={{32,0},{64,32},{96,64},{128,96},{160,128},{192,160},{224,192},{256... | collective-permute-start | bytes 1179656 | tf_op jit(solution)/shard_map/while/body/eval_jaxpr/ppermute | solution.py:12
  567.8 10.5 %collective-permute-start.1 = (bf16[1,2,192,512]{3,2,1,0:T(8,128)(2,1)}, bf16[1,2,192,512]{3,2,1,0:T(8,128)(2,1)S(1)}, u32[]{:S(2)}, u32[]{:S(2)}) collective-permute-start(bf16[1,2,192,512]{3,2,1,0:T(8,128)(2,1)} %get-tuple-element.947), channel_id=1, source_target_pairs={{32,0},{64,32},{96,64},{128,96},{160,128},{192,160},{224,192},{256... | collective-permute-start | bytes 1179656 | tf_op jit(solution)/shard_map/while/body/eval_jaxpr/ppermute | solution.py:12
  579.3 10.5 %collective-permute-start.1 = (bf16[1,2,192,512]{3,2,1,0:T(8,128)(2,1)}, bf16[1,2,192,512]{3,2,1,0:T(8,128)(2,1)S(1)}, u32[]{:S(2)}, u32[]{:S(2)}) collective-permute-start(bf16[1,2,192,512]{3,2,1,0:T(8,128)(2,1)} %get-tuple-element.947), channel_id=1, source_target_pairs={{32,0},{64,32},{96,64},{128,96},{160,128},{192,160},{224,192},{256... | collective-permute-start | bytes 1179656 | tf_op jit(solution)/shard_map/while/body/eval_jaxpr/ppermute | solution.py:12
  590.7 10.5 %collective-permute-start.1 = (bf16[1,2,192,512]{3,2,1,0:T(8,128)(2,1)}, bf16[1,2,192,512]{3,2,1,0:T(8,128)(2,1)S(1)}, u32[]{:S(2)}, u32[]{:S(2)}) collective-permute-start(bf16[1,2,192,512]{3,2,1,0:T(8,128)(2,1)} %get-tuple-element.947), channel_id=1, source_target_pairs={{32,0},{64,32},{96,64},{128,96},{160,128},{192,160},{224,192},{256... | collective-permute-start | bytes 1179656 | tf_op jit(solution)/shard_map/while/body/eval_jaxpr/ppermute | solution.py:12
  602.1 10.5 %collective-permute-start.1 = (bf16[1,2,192,512]{3,2,1,0:T(8,128)(2,1)}, bf16[1,2,192,512]{3,2,1,0:T(8,128)(2,1)S(1)}, u32[]{:S(2)}, u32[]{:S(2)}) collective-permute-start(bf16[1,2,192,512]{3,2,1,0:T(8,128)(2,1)} %get-tuple-element.947), channel_id=1, source_target_pairs={{32,0},{64,32},{96,64},{128,96},{160,128},{192,160},{224,192},{256... | collective-permute-start | bytes 1179656 | tf_op jit(solution)/shard_map/while/body/eval_jaxpr/ppermute | solution.py:12
  613.5 43.2 %collective-permute-start.1 = (bf16[1,2,192,512]{3,2,1,0:T(8,128)(2,1)}, bf16[1,2,192,512]{3,2,1,0:T(8,128)(2,1)S(1)}, u32[]{:S(2)}, u32[]{:S(2)}) collective-permute-start(bf16[1,2,192,512]{3,2,1,0:T(8,128)(2,1)} %get-tuple-element.947), channel_id=1, source_target_pairs={{32,0},{64,32},{96,64},{128,96},{160,128},{192,160},{224,192},{256... | collective-permute-start | bytes 1179656 | tf_op jit(solution)/shard_map/while/body/eval_jaxpr/ppermute | solution.py:12
  662.7 10.5 %collective-permute-start.1 = (bf16[1,2,192,512]{3,2,1,0:T(8,128)(2,1)}, bf16[1,2,192,512]{3,2,1,0:T(8,128)(2,1)S(1)}, u32[]{:S(2)}, u32[]{:S(2)}) collective-permute-start(bf16[1,2,192,512]{3,2,1,0:T(8,128)(2,1)} %get-tuple-element.947), channel_id=1, source_target_pairs={{32,0},{64,32},{96,64},{128,96},{160,128},{192,160},{224,192},{256... | collective-permute-start | bytes 1179656 | tf_op jit(solution)/shard_map/while/body/eval_jaxpr/ppermute | solution.py:12
  679.2 9.3 %collective-permute-start.1 = (bf16[1,2,192,512]{3,2,1,0:T(8,128)(2,1)}, bf16[1,2,192,512]{3,2,1,0:T(8,128)(2,1)S(1)}, u32[]{:S(2)}, u32[]{:S(2)}) collective-permute-start(bf16[1,2,192,512]{3,2,1,0:T(8,128)(2,1)} %get-tuple-element.947), channel_id=1, source_target_pairs={{32,0},{64,32},{96,64},{128,96},{160,128},{192,160},{224,192},{256... | collective-permute-start | bytes 1179656 | tf_op jit(solution)/shard_map/while/body/eval_jaxpr/ppermute | solution.py:12
  689.5 9.3 %collective-permute-start.1 = (bf16[1,2,192,512]{3,2,1,0:T(8,128)(2,1)}, bf16[1,2,192,512]{3,2,1,0:T(8,128)(2,1)S(1)}, u32[]{:S(2)}, u32[]{:S(2)}) collective-permute-start(bf16[1,2,192,512]{3,2,1,0:T(8,128)(2,1)} %get-tuple-element.947), channel_id=1, source_target_pairs={{32,0},{64,32},{96,64},{128,96},{160,128},{192,160},{224,192},{256... | collective-permute-start | bytes 1179656 | tf_op jit(solution)/shard_map/while/body/eval_jaxpr/ppermute | solution.py:12
  (12 other events, 261.5 us)
where the time goes:
time: 771 us; the launch traced here: 757 us
  waiting for transfers between devices  260 us (34%)
  other arithmetic  168 us (22%)
  starting transfers between devices  140 us (18%)
  blocking collectives  131 us (17%)
  local copies, waits for them, and re-layouts  52.3 us (7%)
    ppermute x34, waiting for transfers between devices, shifted_2(): return lax.ppermute(block, axis, route)  260 us
    ppermute x34, starting transfers between devices, shifted_2(): return lax.ppermute(block, axis, route)  130 us
    scatter-add x1, other arithmetic, body(): jax.ops.segment_sum(arrived.T.astype(jnp.float32), flat_index, num_segmen...  107 us
    psum x1, blocking collectives, body(): total_terms = lax.psum(image_terms, 'freq')  58.1 us
    all_gather x1, blocking collectives, body(): lax.all_gather(shot_of_trace, 'freq', axis=0, tiled=True)  37.4 us
    all_gather x1, blocking collectives, body(): lax.all_gather(receiver_cell, 'freq', axis=0, tiled=True)  35.1 us
    convert_element_type x1, other arithmetic, body(): surface = summed.T.astype(jnp.bfloat16)  25.4 us
    another operation x32, local copies, waits for them, and re-layouts  23.4 us
  transfers between devices with their start and end apart: 35, of which 34 were waited for; matrix products, arithmetic and copies ran while one was open for 0% of the time, Pallas kernels for 0%

commit v1 on v0

v1 whole, which is shorter than its diff:
```python
import functools

import jax
import jax.numpy as jnp
from jax import lax
from jax.experimental import pallas as pl
from jax.experimental.pallas import tpu as pltpu
from jax.sharding import PartitionSpec as P

MESH = pl.DeviceIdType.MESH
SHOTS_DEV = 6
SH = 32
F32 = jnp.float32
BF16 = jnp.bfloat16


def product(rows, matrix):
    return jnp.dot(rows, matrix, preferred_element_type=F32)


def lanes(tile, row, width):
    return jnp.concatenate([tile[4 * q + row : 4 * q + row + 1] for q in range(width // 128)], axis=1)


def kernel(
    n_depth,
    n_freq,
    slot_ref,
    traces_ref,
    shot_ref,
    cell_ref,
    slow_ref,
    model_ref,
    oper_ref,
    grad_ref,
    tops_ref,
    opn,
    opt,
    par,
    cosines,
    sines,
    outbox,
    inbox,
    din,
    dout,
    vbuf,
    uin,
    abuf,
    gacc,
    gsend,
    gbox,
    gpair,
    load_sem,
    core_send,
    core_recv,
    box_send,
    box_recv,
    down_send,
    down_recv,
    up_send,
    up_recv,
    tops_local,
    tops_send,
    tops_recv,
    g_send,
    g_recv,
):
    d = lax.axis_index("depth")
    f = lax.axis_index("freq")
    z = d // 2
    c = d % 2
    last = n_depth // 2 - 1
    partner = {"depth": z * 2 + (1 - c)}
    below = {"depth": (d + 2) % n_depth}
    above = {"depth": (d + n_depth - 2) % n_depth}
    chunks = din.shape[0]
    lateral = din.shape[-1]

    barrier = pltpu.get_barrier_semaphore()
    for neighbour in (partner, below, above):
        pl.semaphore_signal(barrier, inc=1, device_id=neighbour, device_id_type=MESH)

    @pl.loop(1, n_freq)
    def _(k):
        pl.semaphore_signal(barrier, inc=1, device_id={"freq": (f + k) % n_freq}, device_id_type=MESH)

    own_copy = pltpu.make_async_copy(oper_ref.at[0, c], opn.at[c], load_sem)
    own_copy.start()

    row8 = lax.broadcasted_iota(jnp.int32, (8, lateral), 0)
    par[c] = jnp.where(row8 == 0, slow_ref[...], model_ref[...])

    @pl.when(z == 0)
    def _():
        rows = outbox.shape[0] * 16
        row = lax.broadcasted_iota(jnp.int32, (rows, 128), 0)
        column = lax.broadcasted_iota(jnp.int32, (rows, 128), 1)
        group, place = row // 16, row % 16
        kind, piece = place % 4, place // 4
        wanted = jnp.where(kind < 2, group * 4 + 2 * c + kind, -1)
        total = jnp.zeros((rows, 128), F32)
        for q in range(4):
            select = jnp.where((column == wanted) & (piece == q), 1.0, 0.0).astype(BF16)
            total += lax.dot_general(
                select,
                traces_ref[128 * q : 128 * (q + 1), :],
                (((1,), (1,)), ((), ())),
                preferred_element_type=F32,
            )
        shot = shot_ref[...]
        cell = cell_ref[...]
        first = (shot * 4 + cell // 128).astype(F32)
        second = (cell % 128).astype(F32)
        row16 = lax.broadcasted_iota(jnp.int32, (16, 128), 0)
        label = jnp.zeros((16, 128), F32)
        for q in range(4):
            label = jnp.where(row16 == 4 * q + 2, first[:, 128 * q : 128 * (q + 1)], label)
            label = jnp.where(row16 == 4 * q + 3, second[:, 128 * q : 128 * (q + 1)], label)
        filled = total.reshape(n_freq, 16, 128) + label[None]
        outbox[...] = filled.astype(BF16)
        inbox[f] = outbox[f]

    pl.semaphore_wait(barrier, n_freq + 2)

    def box_copy(k):
        return pltpu.make_async_remote_copy(
            src_ref=outbox.at[(f + k) % n_freq],
            dst_ref=inbox.at[f],
            send_sem=box_send.at[k],
            recv_sem=box_recv.at[f],
            device_id={"freq": (f + k) % n_freq},
            device_id_type=MESH,
        )

    @pl.when(z == 0)
    def _():
        @pl.loop(1, n_freq)
        def _(k):
            box_copy(k).start()

    def core_copy(source, target, index):
        return pltpu.make_async_remote_copy(
            src_ref=source,
            dst_ref=target,
            send_sem=core_send.at[index],
            recv_sem=core_recv.at[index],
            device_id=partner,
            device_id_type=MESH,
        )

    oper_copy = core_copy(oper_ref.at[0, 1 - c], opn.at[c], 0)
    par_copy = core_copy(par.at[c], par.at[c], 1)
    oper_copy.start()
    par_copy.start()
    oper_wait = core_copy(oper_ref.at[0, 1 - c], opn.at[1 - c], 0)
    par_wait = core_copy(par.at[1 - c], par.at[1 - c], 1)

    own_copy.wait()
    for p in range(2):
        opt[c, p] = opn[c, p].T
    par_wait.wait_recv()
    scale = 0.1 * (slot_ref[c].astype(F32) + 1.0)
    for e in range(2):
        theta = scale * par[e, 0:1, :]
        cosines[e] = jnp.cos(theta)
        sines[e] = jnp.sin(theta)
    oper_wait.wait_recv()
    for p in range(2):
        opt[1 - c, p] = opn[1 - c, p].T
    gacc[...] = jnp.zeros_like(gacc)

    def wait_box(source):
        @pl.when(source != f)
        def _():
            pltpu.make_async_remote_copy(
                src_ref=outbox.at[source],
                dst_ref=inbox.at[source],
                send_sem=box_send.at[source],
                recv_sem=box_recv.at[source],
                device_id={"freq": source},
                device_id_type=MESH,
            ).wait_recv()

    def bin_chunk(j):
        start = SH * j
        first_source = start // SHOTS_DEV
        after = (start + SH - 1) // SHOTS_DEV + 1
        fresh = jnp.where(j == 0, 0, (start - 1) // SHOTS_DEV + 1)

        @pl.loop(fresh, after)
        def _(source):
            wait_box(source)

        row = lax.broadcasted_iota(jnp.int32, (4 * SH, 4 * 128), 0).astype(F32)
        lane_row = lax.broadcasted_iota(jnp.int32, (128, 4 * 128), 0).astype(F32)

        def add_source(source, total):
            tile = inbox[source].astype(F32)
            real, imag = lanes(tile, 0, 512), lanes(tile, 1, 512)
            first, low = lanes(tile, 2, 512), lanes(tile, 3, 512)
            shot = jnp.floor(first * 0.25)
            high = first - 4.0 * shot
            place = shot + (SHOTS_DEV * source - start).astype(F32)
            inside = (place >= 0.0) & (place < float(SH))
            target = jnp.where(inside, high * float(SH) + place, -1.0)
            hit = row == target
            left = jnp.concatenate(
                [jnp.where(hit, real, 0.0).astype(BF16), jnp.where(hit, imag, 0.0).astype(BF16)], axis=0
            )
            right = jnp.where(lane_row == low, 1.0, 0.0).astype(BF16)
            return total + lax.dot_general(left, right, (((1,), (1,)), ((), ())), preferred_element_type=F32)

        total = lax.fori_loop(first_source, after, add_source, jnp.zeros((8 * SH, 128), F32))
        for p in range(2):
            for high in range(4):
                at = (4 * p + high) * SH
                din[j, p, :, 128 * high : 128 * (high + 1)] = total[at : at + SH].astype(BF16)

    def down_copy(j):
        return pltpu.make_async_remote_copy(
            src_ref=dout.at[j],
            dst_ref=din.at[j],
            send_sem=down_send.at[j],
            recv_sem=down_recv.at[j],
            device_id=below,
            device_id_type=MESH,
        )

    def up_copy(j):
        return pltpu.make_async_remote_copy(
            src_ref=abuf.at[0, j],
            dst_ref=uin.at[j],
            send_sem=up_send.at[j],
            recv_sem=up_recv.at[j],
            device_id=above,
            device_id_type=MESH,
        )

    def shift(e, j, real, imag):
        cos_row, sin_row = cosines[e], sines[e]
        shifted_real = (cos_row * real - sin_row * imag).astype(BF16)
        shifted_imag = (cos_row * imag + sin_row * real).astype(BF16)
        vbuf[e, j, 0] = shifted_real
        vbuf[e, j, 1] = shifted_imag
        return jnp.concatenate([shifted_real, shifted_imag], axis=0)

    def forward(e, stacked):
        by_real = product(stacked, opt[e, 0])
        by_imag = product(stacked, opt[e, 1])
        return (by_real[:SH] - by_imag[SH:]).astype(BF16), (by_imag[:SH] + by_real[SH:]).astype(BF16)

    def down(j):
        @pl.when(z == 0)
        def _():
            bin_chunk(j)

        @pl.when(z > 0)
        def _():
            down_copy(j).wait_recv()

        stacked = shift(0, j, din[j, 0].astype(F32), din[j, 1].astype(F32))
        real, imag = forward(0, stacked)
        stacked = shift(1, j, real.astype(F32), imag.astype(F32))

        @pl.when(z < last)
        def _():
            real, imag = forward(1, stacked)
            dout[j, 0] = real
            dout[j, 1] = imag
            down_copy(j).start()

    def tops_here(e, j):
        return pltpu.make_async_copy(
            abuf.at[e, j], tops_ref.at[0, c, :, pl.ds(pl.multiple_of(j * SH, SH), SH), :], tops_local.at[j]
        )

    def tops_there(e, j, slot):
        return pltpu.make_async_remote_copy(
            src_ref=abuf.at[e, j],
            dst_ref=tops_ref.at[0, slot, :, pl.ds(pl.multiple_of(j * SH, SH), SH), :],
            send_sem=tops_send.at[j],
            recv_sem=tops_recv.at[j],
            device_id=partner,
            device_id_type=MESH,
        )

    def backward(e, j, real, imag):
        old_real, old_imag = vbuf[e, j, 0].astype(F32), vbuf[e, j, 1].astype(F32)
        model = par[e, 1:2, :]
        source_real = real + model * old_real
        source_imag = imag + model * old_imag
        term = old_real * source_real + old_imag * source_imag
        gacc[e] += jnp.sum(term.reshape(SH // 8, 8, lateral), axis=0)
        stacked = jnp.concatenate([source_real.astype(BF16), source_imag.astype(BF16)], axis=0)
        by_real = product(stacked, opn[e, 0])
        by_imag = product(stacked, opn[e, 1])
        back_real = by_real[:SH] + by_imag[SH:]
        back_imag = by_real[SH:] - by_imag[:SH]
        cos_row, sin_row = cosines[e], sines[e]
        out_real = (cos_row * back_real + sin_row * back_imag).astype(BF16)
        out_imag = (cos_row * back_imag - sin_row * back_real).astype(BF16)
        abuf[e, j, 0] = out_real
        abuf[e, j, 1] = out_imag

        if e == 0:
            @pl.when(z > 0)
            def _():
                up_copy(j).start()

        @pl.when(c == e)
        def _():
            tops_here(e, j).start()

        @pl.when(c != e)
        def _():
            tops_there(e, j, c).start()

        return out_real, out_imag

    def up(j):
        @pl.when(z < last)
        def _():
            up_copy(j).wait_recv()

        real, imag = backward(1, j, uin[j, 0].astype(F32), uin[j, 1].astype(F32))
        backward(0, j, real.astype(F32), imag.astype(F32))

    @pl.when(z == last)
    def _():
        uin[...] = jnp.zeros_like(uin)

    @pl.loop(0, chunks)
    def _(j):
        down(j)

        @pl.when(z == last)
        def _():
            up(j)

    @pl.when(z < last)
    def _():
        @pl.loop(0, chunks)
        def _(j):
            up(j)

    row8 = lax.broadcasted_iota(jnp.int32, (8, 128), 0)
    tile = jnp.zeros((8, 128), F32)
    for e in range(2):
        summed = jnp.sum(gacc[e], axis=0, keepdims=True)
        for q in range(4):
            tile = jnp.where(row8 == 4 * e + q, summed[:, 128 * q : 128 * (q + 1)], tile)
    gsend[...] = tile

    def g_copy(k):
        return pltpu.make_async_remote_copy(
            src_ref=gsend,
            dst_ref=gbox.at[f],
            send_sem=g_send.at[k],
            recv_sem=g_recv.at[f],
            device_id={"freq": (f + k) % n_freq},
            device_id_type=MESH,
        )

    @pl.loop(1, n_freq)
    def _(k):
        g_copy(k).start()

    gbox[f] = tile

    @pl.loop(1, n_freq)
    def _(k):
        source = (f + k) % n_freq
        pltpu.make_async_remote_copy(
            src_ref=gsend,
            dst_ref=gbox.at[source],
            send_sem=g_send.at[k],
            recv_sem=g_recv.at[source],
            device_id={"freq": source},
            device_id_type=MESH,
        ).wait_recv()

    gpair[0] = jnp.sum(gbox[...], axis=0)
    pair_copy = core_copy(gpair.at[0], gpair.at[1], 2)
    pair_copy.start()
    pair_copy.wait_recv()
    both = gpair[0] + gpair[1]
    mine = jnp.where(c == 0, both[0:4], both[4:8]) * (1.0 / (2.0 * n_freq * SHOTS_DEV * n_freq))
    grad_ref[...] = jnp.concatenate([mine[q : q + 1] for q in range(4)], axis=1)

    pair_copy.wait_send()
    oper_copy.wait_send()
    par_copy.wait_send()

    @pl.loop(1, n_freq)
    def _(k):
        g_copy(k).wait_send()

    @pl.when(z == 0)
    def _():
        @pl.loop(1, n_freq)
        def _(k):
            box_copy(k).wait_send()

    @pl.loop(0, chunks)
    def _(j):
        @pl.when(z < last)
        def _():
            down_copy(j).wait_send()

        @pl.when(z > 0)
        def _():
            up_copy(j).wait_send()

        tops_here(c, j).wait()
        tops_there(1 - c, j, c).wait_send()
        tops_there(1 - c, j, 1 - c).wait_recv()


def body(traces, shot_of_trace, receiver_cell, slot_freq, operators, slowness, image_model):
    n_freq = lax.axis_size("freq")
    n_depth = lax.axis_size("depth")
    local_freqs = operators.shape[1]
    lateral = operators.shape[-1]
    shot_total = SHOTS_DEV * n_freq
    chunks = shot_total // SH
    block = (2, SH, lateral)
    vmem = pl.BlockSpec(memory_space=pltpu.VMEM)
    dma = pltpu.SemaphoreType.DMA
    gradient, tops = pl.pallas_call(
        functools.partial(kernel, n_depth, n_freq),
        out_shape=(
            jax.ShapeDtypeStruct((1, lateral), F32),
            jax.ShapeDtypeStruct((1, local_freqs, 2, shot_total, lateral), BF16),
        ),
        in_specs=[pl.BlockSpec(memory_space=pltpu.SMEM)] + [vmem] * 5 + [pl.BlockSpec(memory_space=pl.ANY)],
        out_specs=(vmem, pl.BlockSpec(memory_space=pl.ANY)),
        scratch_shapes=[
            pltpu.VMEM((2, 2, lateral, lateral), BF16),
            pltpu.VMEM((2, 2, lateral, lateral), BF16),
            pltpu.VMEM((2, 8, lateral), F32),
            pltpu.VMEM((2, 1, lateral), F32),
            pltpu.VMEM((2, 1, lateral), F32),
            pltpu.VMEM((n_freq, 16, 128), BF16),
            pltpu.VMEM((n_freq, 16, 128), BF16),
            pltpu.VMEM((chunks,) + block, BF16),
            pltpu.VMEM((chunks,) + block, BF16),
            pltpu.VMEM((2, chunks) + block, BF16),
            pltpu.VMEM((chunks,) + block, BF16),
            pltpu.VMEM((2, chunks) + block, BF16),
            pltpu.VMEM((2, 8, lateral), F32),
            pltpu.VMEM((8, 128), F32),
            pltpu.VMEM((n_freq, 8, 128), F32),
            pltpu.VMEM((2, 8, 128), F32),
            dma(()),
            dma((3,)),
            dma((3,)),
            dma((n_freq,)),
            dma((n_freq,)),
            dma((chunks,)),
            dma((chunks,)),
            dma((chunks,)),
            dma((chunks,)),
            dma((chunks,)),
            dma((chunks,)),
            dma((chunks,)),
            dma((n_freq,)),
            dma((n_freq,)),
        ],
        compiler_params=pltpu.CompilerParams(
            collective_id=0, has_side_effects=True, vmem_limit_bytes=48 * 2**20
        ),
        cost_estimate=pl.CostEstimate(flops=2 * 10**9, bytes_accessed=4 * 10**6, transcendentals=4096),
        name="migrate",
    )(slot_freq, traces, shot_of_trace, receiver_cell, slowness, image_model, operators)
    return gradient, tops


def solution(mesh):
    in_specs = (
        P("freq", None),
        P("freq", None),
        P("freq", None),
        P("freq"),
        P("depth", "freq", None, None, None),
        P("depth", None),
        P("depth", None),
    )
    out_specs = (P("depth", None), P("depth", "freq", None, None, None))
    return jax.shard_map(body, mesh=mesh, in_specs=in_specs, out_specs=out_specs, check_vma=False)
```

time: 771 us -> 105 us (0.14); the launches traced: 757 us -> 105 us
  waiting for transfers between devices: 260 us -> 0 us
  other arithmetic: 168 us -> 0 us
  starting transfers between devices: 140 us -> 0 us
  blocking collectives: 131 us -> 0 us
  Pallas kernels: 0 us -> 96.9 us
  local copies, waits for them, and re-layouts: 52.3 us -> 7.33 us
    ppermute x34 -> x0, waiting for transfers between devices: 260 us -> none  [shifted_2(): return lax.ppermute(block, axis, route)]
    ppermute x34 -> x0, starting transfers between devices: 130 us -> none  [shifted_2(): return lax.ppermute(block, axis, route)]
    scatter-add x1 -> x0, other arithmetic: 107 us -> none  [body(): jax.ops.segment_sum(arrived.T.astype(jnp.float32), flat_index, num_segmen...]
    pallas_call x0 -> x1, Pallas kernels: none -> 96.9 us  [body(): pl.pallas_call(functools.partial(kernel, n_depth, n_freq), out_shape=(jax...]
    all_gather x2 -> x0, blocking collectives: 72.4 us -> none  [the longest x1 37.4 us: body(): lax.all_gather(shot_of_trace, 'freq', axis=0, tiled=True)]
    psum x1 -> x0, blocking collectives: 58.1 us -> none  [body(): total_terms = lax.psum(image_terms, 'freq')]
    convert_element_type x40 -> x0, other arithmetic: 51 us -> none  [the longest x1 25.4 us: body(): surface = summed.T.astype(jnp.bfloat16)]
    convert_element_type x2 -> x0, local copies, waits for them, and re-layouts: 23.5 us -> none  [the longest x1 18.5 us: body(): surface = summed.T.astype(jnp.bfloat16)]
  transfers between devices with their start and end apart: 35 -> 0, of which waited for: 34 -> 0; matrix products, arithmetic and copies ran while one was open for 0% -> 0% of each run, Pallas kernels for 0% -> 0%
where the time goes in v1:
time: 105 us
  Pallas kernels  96.9 us (92%)
  local copies, waits for them, and re-layouts  7.33 us (7%)
    pallas_call x1, Pallas kernels, body(): pl.pallas_call(functools.partial(kernel, n_depth, n_freq), out_shape=(jax...  96.9 us
    unnamed x16, local copies, waits for them, and re-layouts  7.33 us

profile of v1, /device:TPU:1, one launch (start us, length us, event | category | flops | bytes accessed | tf_op | source)
XLA Modules:
  0.0 104.9 jit_solution(7888319474352653585)
XLA Ops:
  0.6 0.0 copy-start
  0.6 1.6 %copy-done = bf16[1,2,2,512,512]{4,3,2,1,0:T(8,128)(2,1)S(1)} copy-done((bf16[1,2,2,512,512]{4,3,2,1,0:T(8,128)(2,1)S(1)}, bf16[1,2,2,512,512]{4,3,2,1,0:T(8,128)(2,1)}, u32[]{:S(2)}) %copy-start) | copy-done | bytes 2097176
  2.2 0.0 copy-start.1
  2.2 0.9 copy-done.1
  3.1 0.0 copy-start.2
  3.1 0.7 copy-done.2
  3.8 0.0 copy-start.3
  3.8 0.7 copy-done.3
  4.5 0.0 copy-start.4
  4.5 0.7 copy-done.4
  5.2 0.0 copy-start.5
  5.2 0.7 copy-done.5
  5.9 0.0 copy-start.6
  5.9 0.7 copy-done.6
  6.5 96.9 %migrate.1 = (f32[1,512]{1,0:T(1,128)S(1)}, bf16[1,2,2,192,512]{4,3,2,1,0:T(8,128)(2,1)S(1)}) custom-call(s32[2]{0:T(128)S(1)} %copy-done.6, bf16[512,128]{1,0:T(8,128)(2,1)S(1)} %copy-done.1, s32[1,512]{1,0:T(1,128)S(1)} %copy-done.2, s32[1,512]{1,0:T(1,128)S(1)} %copy-done.3, f32[1,512]{1,0:T(1,128)S(1)} %copy-done.4, f32[1,512]{1,0:T(1,128)S(1)} %copy-done.5, ...), custom_call_target="tpu_custom_call" | custom-call | flops 2000000000 | bytes 4000000 | tf_op jit(solution)/shard_map/migrate/pallas_call | solution.py:429
  103.4 0.6 copy.11
  104.0 0.9 copy.12
Async XLA Ops:
  0.6 1.6 %copy-start = (bf16[1,2,2,512,512]{4,3,2,1,0:T(8,128)(2,1)S(1)}, bf16[1,2,2,512,512]{4,3,2,1,0:T(8,128)(2,1)}, u32[]{:S(2)}) copy-start(bf16[1,2,2,512,512]{4,3,2,1,0:T(8,128)(2,1)} %oper_ref.1) | copy-start | bytes 6291460
  2.2 0.9 copy-start.1
  3.1 0.7 copy-start.2
  3.8 0.7 copy-start.3
  4.5 0.7 copy-start.4
  5.2 0.7 copy-start.5
  5.9 0.7 copy-start.6

commit v2 on v1

v2 whole, which is shorter than its diff:
```python
import functools

import jax
import jax.numpy as jnp
from jax import lax
from jax.experimental import pallas as pl
from jax.experimental.pallas import tpu as pltpu
from jax.sharding import PartitionSpec as P

MESH = pl.DeviceIdType.MESH
SHOTS_DEV = 6
SH = 32
SINGLES = 4
F32 = jnp.float32
BF16 = jnp.bfloat16


def product(rows, matrix):
    return jnp.dot(rows, matrix, preferred_element_type=F32)


def product_rows(rows, matrix):
    return lax.dot_general(rows, matrix, (((1,), (1,)), ((), ())), preferred_element_type=F32)


def lanes(tile, row, width):
    return jnp.concatenate([tile[4 * q + row : 4 * q + row + 1] for q in range(width // 128)], axis=1)


def kernel(
    n_depth,
    n_freq,
    slot_hbm,
    traces_hbm,
    shot_hbm,
    cell_hbm,
    slow_hbm,
    model_hbm,
    oper_ref,
    grad_ref,
    tops_ref,
    slot_ref,
    traces_ref,
    shot_ref,
    cell_ref,
    slow_ref,
    model_ref,
    opn,
    opt,
    par,
    cosines,
    sines,
    outbox,
    inbox,
    bins,
    din,
    dout,
    vbuf,
    uin,
    abuf,
    gacc,
    gpart,
    gin,
    gsend,
    gbox,
    load_sem,
    oper_send,
    oper_recv,
    par_send,
    par_recv,
    box_send,
    box_recv,
    down_send,
    down_recv,
    up_send,
    up_recv,
    tops_local,
    tops_send,
    tops_recv,
    part_send,
    part_recv,
    g_send,
    g_recv,
):
    d = lax.axis_index("depth")
    f = lax.axis_index("freq")
    z = d // 2
    c = d % 2
    chunks = din.shape[0]
    lateral = din.shape[-1]
    single = z < SINGLES
    paired = z >= SINGLES
    final = z >= n_depth // 2 - 2
    side = z % 2
    slot = jnp.where(single, c, side)
    rank = jnp.where(single, c, 2 * side + c)
    base = d - rank
    mine = jnp.where(single, chunks, chunks // 2)
    partner = base + jnp.where(single, 1 - c, 2 * side + 1 - c)
    across = base + 2 * (1 - side) + c
    across_other = base + 2 * (1 - side) + 1 - c
    edge = 2 * SINGLES

    def at(depth):
        return {"depth": depth}

    def place_of(turn):
        return jnp.where(single, turn, 2 * turn + c)

    first_chunk = (f * SHOTS_DEV) // SH

    def chunk_of(place):
        return (first_chunk + place) % chunks

    def down_target(place):
        return jnp.where(z < SINGLES - 1, d + 2, jnp.where(single, edge + 2 * c + place % 2, (d + 4) % n_depth))

    up_target = jnp.where(single, (d + n_depth - 2) % n_depth, jnp.where(z < SINGLES + 2, edge - 2 + side, d - 4))

    barrier = pltpu.get_barrier_semaphore()

    def greet(depth):
        pl.semaphore_signal(barrier, inc=1, device_id=at(depth), device_id_type=MESH)

    @pl.loop(1, n_freq)
    def _(k):
        pl.semaphore_signal(barrier, inc=1, device_id={"freq": (f + k) % n_freq}, device_id_type=MESH)

    greet(partner)

    @pl.when(z > 0)
    def _():
        greet(up_target)

    @pl.when(jnp.logical_not(final))
    def _():
        greet(down_target(0))

    @pl.when(z == SINGLES - 1)
    def _():
        greet(down_target(1))

    @pl.when(paired)
    def _():
        greet(across)
        greet(across_other)

    greeted = (
        n_freq
        + jnp.where(z > 0, 1, 0)
        + jnp.where(final, 0, 1)
        + jnp.where(z == SINGLES - 1, 1, 0)
        + jnp.where(paired, 2, 0)
    )

    loads = [
        pltpu.make_async_copy(source, target, load_sem.at[i])
        for i, (source, target) in enumerate(
            [
                (slow_hbm, slow_ref),
                (model_hbm, model_ref),
                (slot_hbm, slot_ref),
                (traces_hbm, traces_ref),
                (shot_hbm, shot_ref),
                (cell_hbm, cell_ref),
                (oper_ref.at[0, slot], opn.at[rank]),
            ]
        )
    ]

    @pl.when(z == 0)
    def _():
        for load in loads[3:6]:
            load.start()

    for load in loads[:3] + loads[6:]:
        load.start()
    for load in loads[:2]:
        load.wait()

    row8 = lax.broadcasted_iota(jnp.int32, (8, lateral), 0)
    par[rank] = jnp.where(row8 == 0, slow_ref[...], model_ref[...])

    @pl.when(z == 0)
    def _():
        for load in loads[3:6]:
            load.wait()
        rows = n_freq * 16
        row = lax.broadcasted_iota(jnp.int32, (rows, 128), 0)
        column = lax.broadcasted_iota(jnp.int32, (rows, 128), 1)
        group, within = row // 16, row % 16
        kind, piece = within % 4, within // 4
        wanted = jnp.where(kind < 2, group * 4 + 2 * c + kind, -1)
        total = jnp.zeros((rows, 128), F32)
        for q in range(4):
            select = jnp.where((column == wanted) & (piece == q), 1.0, 0.0).astype(BF16)
            total += lax.dot_general(
                select,
                traces_ref[128 * q : 128 * (q + 1), :],
                (((1,), (1,)), ((), ())),
                preferred_element_type=F32,
            )
        cell = cell_ref[...]
        first = (cell // 128 * 8 + shot_ref[...]).astype(F32)
        second = (cell % 128).astype(F32)
        row16 = lax.broadcasted_iota(jnp.int32, (16, 128), 0)
        label = jnp.zeros((16, 128), F32)
        for q in range(4):
            label = jnp.where(row16 == 4 * q + 2, first[:, 128 * q : 128 * (q + 1)], label)
            label = jnp.where(row16 == 4 * q + 3, second[:, 128 * q : 128 * (q + 1)], label)
        filled = total.reshape(n_freq, 16, 128) + label[None]
        outbox[...] = filled.astype(BF16)
        inbox[f] = outbox[f]

    pl.semaphore_wait(barrier, greeted)

    def box_copy(k):
        return pltpu.make_async_remote_copy(
            src_ref=outbox.at[(f + k) % n_freq],
            dst_ref=inbox.at[f],
            send_sem=box_send.at[k],
            recv_sem=box_recv.at[f],
            device_id={"freq": (f + k) % n_freq},
            device_id_type=MESH,
        )

    @pl.when(z == 0)
    def _():
        @pl.loop(1, n_freq // 2)
        def _(k):
            box_copy(k).start()
            box_copy(n_freq - k).start()

        box_copy(n_freq // 2).start()

    def par_copy(mate, index, target):
        return pltpu.make_async_remote_copy(
            src_ref=par.at[index],
            dst_ref=par.at[index],
            send_sem=par_send.at[mate],
            recv_sem=par_recv.at[index],
            device_id=at(target),
            device_id_type=MESH,
        )

    def oper_copy(source, index, send, target):
        return pltpu.make_async_remote_copy(
            src_ref=source,
            dst_ref=opn.at[index],
            send_sem=oper_send.at[send],
            recv_sem=oper_recv.at[index, 0],
            device_id=at(target),
            device_id_type=MESH,
        )

    def half_copy(source, index, p, send, target):
        return pltpu.make_async_remote_copy(
            src_ref=source,
            dst_ref=opn.at[index, p],
            send_sem=oper_send.at[send],
            recv_sem=oper_recv.at[index, p],
            device_id=at(target),
            device_id_type=MESH,
        )

    partner_rank = partner - base
    across_rank = across - base
    other_rank = across_other - base
    to_partner = oper_copy(oper_ref.at[0, jnp.where(single, 1 - c, side)], rank, 0, partner)
    from_partner = oper_copy(oper_ref.at[0, slot], partner_rank, 0, partner)

    @pl.when(paired)
    def _():
        for p in range(2):
            half_copy(oper_ref.at[0, 1 - side, p], rank, p, 1 + p, across).start()

    par_copy(0, rank, partner).start()
    to_partner.start()

    @pl.when(paired)
    def _():
        par_copy(1, rank, across).start()
        par_copy(2, rank, across_other).start()

    loads[2].wait()
    loads[6].wait()
    scale = 0.1 * (slot_ref[slot].astype(F32) + 1.0)

    def angles(e):
        theta = scale * par[e, 0:1, :]
        cosines[e] = jnp.cos(theta)
        sines[e] = jnp.sin(theta)

    gacc[...] = jnp.zeros_like(gacc)

    @pl.when(single)
    def _():
        for p in range(2):
            opt[rank, p] = opn[rank, p].T

    par_copy(0, partner_rank, partner).wait_recv()
    angles(rank)
    angles(partner_rank)
    from_partner.wait_recv()

    @pl.when(single)
    def _():
        for p in range(2):
            opt[partner_rank, p] = opn[partner_rank, p].T

    @pl.when(paired)
    def _():
        par_copy(1, across_rank, across).wait_recv()
        par_copy(2, other_rank, across_other).wait_recv()
        angles(across_rank)
        angles(other_rank)
        for p in range(2):
            half_copy(oper_ref.at[0, slot, p], across_rank, p, 1 + p, across).wait_recv()
            half_copy(opn.at[across_rank, p], across_rank, p, 3 + p, partner).start()
        for p in range(2):
            half_copy(opn.at[other_rank, p], other_rank, p, 3 + p, partner).wait_recv()

    def wait_box(source):
        @pl.when(source != f)
        def _():
            pltpu.make_async_remote_copy(
                src_ref=outbox.at[source],
                dst_ref=inbox.at[source],
                send_sem=box_send.at[source],
                recv_sem=box_recv.at[source],
                device_id={"freq": source},
                device_id_type=MESH,
            ).wait_recv()

    sources = max((SH * j + SH - 1) // SHOTS_DEV - SH * j // SHOTS_DEV + 1 for j in range(chunks))

    def bin_chunk(place):
        j = chunk_of(place)
        start = SH * j
        first_source = start // SHOTS_DEV
        fresh = jnp.where(place == 0, first_source, (start + SHOTS_DEV - 1) // SHOTS_DEV)
        after = jnp.where(
            (place == chunks - 1) & (first_chunk > 0),
            (SH * first_chunk) // SHOTS_DEV,
            (start + SH - 1) // SHOTS_DEV + 1,
        )

        @pl.loop(fresh, after)
        def _(source):
            wait_box(source)

        top = 8 + SHOTS_DEV * first_source - start
        row = lax.broadcasted_iota(jnp.int32, (32, 4 * 128), 0).astype(F32)
        lane_row = lax.broadcasted_iota(jnp.int32, (128, 4 * 128), 0).astype(F32)
        for i in range(sources):
            tile = inbox[first_source + i].astype(F32)
            real, imag = lanes(tile, 0, 512), lanes(tile, 1, 512)
            first, low = lanes(tile, 2, 512), lanes(tile, 3, 512)
            hit = row == first
            left = jnp.concatenate(
                [jnp.where(hit, real, 0.0).astype(BF16), jnp.where(hit, imag, 0.0).astype(BF16)], axis=0
            )
            right = jnp.where(lane_row == low, 1.0, 0.0).astype(BF16)
            part = lax.dot_general(left, right, (((1,), (1,)), ((), ())), preferred_element_type=F32)
            for g in range(8):
                bins[g, pl.ds(top + SHOTS_DEV * i, 8), :] = part[8 * g : 8 * (g + 1)]
        for p in range(2):
            for high in range(4):
                din[place, p, :, 128 * high : 128 * (high + 1)] = bins[4 * p + high, 8 : 8 + SH, :].astype(BF16)

    def down_copy(place):
        return pltpu.make_async_remote_copy(
            src_ref=dout.at[place],
            dst_ref=din.at[place],
            send_sem=down_send.at[place],
            recv_sem=down_recv.at[place],
            device_id=at(down_target(place)),
            device_id_type=MESH,
        )

    def up_copy(place):
        return pltpu.make_async_remote_copy(
            src_ref=abuf.at[0, place],
            dst_ref=uin.at[place],
            send_sem=up_send.at[place],
            recv_sem=up_recv.at[place],
            device_id=at(up_target),
            device_id_type=MESH,
        )

    def shift(e, place, real, imag):
        cos_row, sin_row = cosines[e], sines[e]
        shifted_real = (cos_row * real - sin_row * imag).astype(BF16)
        shifted_imag = (cos_row * imag + sin_row * real).astype(BF16)
        vbuf[e, place, 0] = shifted_real
        vbuf[e, place, 1] = shifted_imag
        return jnp.concatenate([shifted_real, shifted_imag], axis=0)

    def forward(stacked, by_real, by_imag):
        return (by_real[:SH] - by_imag[SH:]).astype(BF16), (by_imag[:SH] + by_real[SH:]).astype(BF16)

    def forward_single(e, stacked):
        return forward(stacked, product(stacked, opt[e, 0]), product(stacked, opt[e, 1]))

    def forward_pair(e, stacked):
        return forward(stacked, product_rows(stacked, opn[e, 0]), product_rows(stacked, opn[e, 1]))

    def send_down(place, real, imag):
        dout[place, 0] = real
        dout[place, 1] = imag
        down_copy(place).start()

    def down_single(place):
        stacked = shift(0, place, din[place, 0].astype(F32), din[place, 1].astype(F32))
        real, imag = forward_single(0, stacked)
        stacked = shift(1, place, real.astype(F32), imag.astype(F32))
        real, imag = forward_single(1, stacked)
        send_down(place, real, imag)

    def down_pair(place):
        real, imag = din[place, 0], din[place, 1]
        for e in range(3):
            stacked = shift(e, place, real.astype(F32), imag.astype(F32))
            real, imag = forward_pair(e, stacked)
        stacked = shift(3, place, real.astype(F32), imag.astype(F32))

        @pl.when(jnp.logical_not(final))
        def _():
            real, imag = forward_pair(3, stacked)
            send_down(place, real, imag)

    def rows_of(place):
        return pl.ds(pl.multiple_of(chunk_of(place) * SH, SH), SH)

    def tops_here(e, place):
        return pltpu.make_async_copy(abuf.at[e, place], tops_ref.at[0, slot, :, rows_of(place), :], tops_local.at[place])

    def tops_there(e, place, its_slot):
        return pltpu.make_async_remote_copy(
            src_ref=abuf.at[e, place],
            dst_ref=tops_ref.at[0, its_slot, :, rows_of(place), :],
            send_sem=tops_send.at[e, place],
            recv_sem=tops_recv.at[its_slot, place],
            device_id=at(base + e),
            device_id_type=MESH,
        )

    def backward(e, place, real, imag):
        old_real, old_imag = vbuf[e, place, 0].astype(F32), vbuf[e, place, 1].astype(F32)
        model = par[e, 1:2, :]
        source_real = real + model * old_real
        source_imag = imag + model * old_imag
        term = old_real * source_real + old_imag * source_imag
        gacc[e] += jnp.sum(term.reshape(SH // 8, 8, lateral), axis=0)
        stacked = jnp.concatenate([source_real.astype(BF16), source_imag.astype(BF16)], axis=0)
        by_real = product(stacked, opn[e, 0])
        by_imag = product(stacked, opn[e, 1])
        back_real = by_real[:SH] + by_imag[SH:]
        back_imag = by_real[SH:] - by_imag[:SH]
        cos_row, sin_row = cosines[e], sines[e]
        out_real = (cos_row * back_real + sin_row * back_imag).astype(BF16)
        out_imag = (cos_row * back_imag - sin_row * back_real).astype(BF16)
        abuf[e, place, 0] = out_real
        abuf[e, place, 1] = out_imag

        if e == 0:

            @pl.when(z > 0)
            def _():
                up_copy(place).start()

        @pl.when(rank == e)
        def _():
            tops_here(e, place).start()

        @pl.when(rank != e)
        def _():
            tops_there(e, place, slot).start()

        return out_real.astype(F32), out_imag.astype(F32)

    def up(place, steps):
        real, imag = uin[place, 0].astype(F32), uin[place, 1].astype(F32)
        for e in reversed(range(steps)):
            real, imag = backward(e, place, real, imag)

    @pl.when(single)
    def _():
        @pl.loop(0, chunks)
        def _(place):
            @pl.when(z == 0)
            def _():
                bin_chunk(place)

            @pl.when(z > 0)
            def _():
                down_copy(place).wait_recv()

            down_single(place)

        @pl.loop(0, chunks)
        def _(place):
            up_copy(place).wait_recv()
            up(place, 2)

    @pl.when(final)
    def _():
        uin[...] = jnp.zeros_like(uin)

    @pl.when(paired)
    def _():
        @pl.loop(0, 2 * mine)
        def _(turn):
            going_down = jnp.where(final, turn % 2 == 0, turn < mine)
            place = place_of(jnp.where(final, turn // 2, turn % mine))

            @pl.when(going_down)
            def _():
                down_copy(place).wait_recv()
                down_pair(place)

            @pl.when(jnp.logical_not(going_down))
            def _():
                @pl.when(jnp.logical_not(final))
                def _():
                    up_copy(place).wait_recv()

                up(place, 4)

    row4 = lax.broadcasted_iota(jnp.int32, (4, 128), 0)

    def rows_tile(summed):
        tile = jnp.zeros((4, 128), F32)
        for q in range(4):
            tile = jnp.where(row4 == q, summed[:, 128 * q : 128 * (q + 1)], tile)
        return tile

    def part_copy(e, sender):
        return pltpu.make_async_remote_copy(
            src_ref=gpart.at[e],
            dst_ref=gin.at[sender],
            send_sem=part_send.at[e],
            recv_sem=part_recv.at[sender],
            device_id=at(base + e),
            device_id_type=MESH,
        )

    def share(steps):
        for e in range(steps):
            gpart[e] = rows_tile(jnp.sum(gacc[e], axis=0, keepdims=True))

            @pl.when(rank != e)
            def _():
                part_copy(e, rank).start()

        total = gpart[rank]
        for e in range(steps):

            @pl.when(rank != e)
            def _():
                part_copy(e, e).wait_recv()

            @pl.when(rank == e)
            def _():
                gin[e] = jnp.zeros((4, 128), F32)

        for e in range(steps):
            total = total + gin[e]
        gsend[...] = total
        gbox[f] = total

    @pl.when(single)
    def _():
        share(2)

    @pl.when(paired)
    def _():
        share(4)

    def g_copy(k):
        return pltpu.make_async_remote_copy(
            src_ref=gsend,
            dst_ref=gbox.at[f],
            send_sem=g_send.at[k],
            recv_sem=g_recv.at[f],
            device_id={"freq": (f + k) % n_freq},
            device_id_type=MESH,
        )

    @pl.loop(1, n_freq)
    def _(k):
        g_copy(k).start()

    @pl.loop(1, n_freq)
    def _(k):
        source = (f + k) % n_freq
        pltpu.make_async_remote_copy(
            src_ref=gsend,
            dst_ref=gbox.at[source],
            send_sem=g_send.at[k],
            recv_sem=g_recv.at[source],
            device_id={"freq": source},
            device_id_type=MESH,
        ).wait_recv()

    total = jnp.sum(gbox[...], axis=0) * (1.0 / (2.0 * n_freq * SHOTS_DEV * n_freq))
    grad_ref[...] = jnp.concatenate([total[q : q + 1] for q in range(4)], axis=1)

    to_partner.wait_send()
    par_copy(0, rank, partner).wait_send()

    @pl.when(paired)
    def _():
        par_copy(1, rank, across).wait_send()
        par_copy(2, rank, across_other).wait_send()
        for p in range(2):
            half_copy(oper_ref.at[0, 1 - side, p], rank, p, 1 + p, across).wait_send()
            half_copy(opn.at[across_rank, p], across_rank, p, 3 + p, partner).wait_send()

    @pl.loop(1, n_freq)
    def _(k):
        g_copy(k).wait_send()

    @pl.when(z == 0)
    def _():
        @pl.loop(1, n_freq)
        def _(k):
            box_copy(k).wait_send()

    steps = jnp.where(single, 2, 4)

    @pl.loop(0, steps)
    def _(e):
        @pl.when(rank != e)
        def _():
            part_copy(e, rank).wait_send()

            @pl.loop(0, mine)
            def _(turn):
                tops_there(e, place_of(turn), slot).wait_send()

    @pl.loop(0, mine)
    def _(turn):
        place = place_of(turn)

        @pl.when(jnp.logical_not(final))
        def _():
            down_copy(place).wait_send()

        @pl.when(z > 0)
        def _():
            up_copy(place).wait_send()

        tops_here(rank, place).wait()

    @pl.loop(0, 2 * chunks)
    def _(index):
        its_slot, place = index // chunks, index % chunks
        sender = jnp.where(single, its_slot, 2 * its_slot + place % 2)

        @pl.when(sender != rank)
        def _():
            tops_there(rank, place, its_slot).wait_recv()


def body(traces, shot_of_trace, receiver_cell, slot_freq, operators, slowness, image_model):
    n_freq = lax.axis_size("freq")
    n_depth = lax.axis_size("depth")
    local_freqs = operators.shape[1]
    lateral = operators.shape[-1]
    shot_total = SHOTS_DEV * n_freq
    chunks = shot_total // SH
    block = (2, SH, lateral)
    vmem = pl.BlockSpec(memory_space=pltpu.VMEM)
    dma = pltpu.SemaphoreType.DMA
    gradient, tops = pl.pallas_call(
        functools.partial(kernel, n_depth, n_freq),
        out_shape=(
            jax.ShapeDtypeStruct((1, lateral), F32),
            jax.ShapeDtypeStruct((1, local_freqs, 2, shot_total, lateral), BF16),
        ),
        in_specs=[pl.BlockSpec(memory_space=pltpu.HBM)] * 7,
        out_specs=(vmem, pl.BlockSpec(memory_space=pl.ANY)),
        scratch_shapes=[
            pltpu.SMEM(slot_freq.shape, jnp.int32),
            pltpu.VMEM(traces.shape, BF16),
            pltpu.VMEM(shot_of_trace.shape, jnp.int32),
            pltpu.VMEM(receiver_cell.shape, jnp.int32),
            pltpu.VMEM(slowness.shape, F32),
            pltpu.VMEM(image_model.shape, F32),
            pltpu.VMEM((4, 2, lateral, lateral), BF16),
            pltpu.VMEM((2, 2, lateral, lateral), BF16),
            pltpu.VMEM((4, 8, lateral), F32),
            pltpu.VMEM((4, 1, lateral), F32),
            pltpu.VMEM((4, 1, lateral), F32),
            pltpu.VMEM((n_freq, 16, 128), BF16),
            pltpu.VMEM((n_freq, 16, 128), BF16),
            pltpu.VMEM((8, SH + 32, 128), F32),
            pltpu.VMEM((chunks,) + block, BF16),
            pltpu.VMEM((chunks,) + block, BF16),
            pltpu.VMEM((4, chunks) + block, BF16),
            pltpu.VMEM((chunks,) + block, BF16),
            pltpu.VMEM((4, chunks) + block, BF16),
            pltpu.VMEM((4, 8, lateral), F32),
            pltpu.VMEM((4, 4, 128), F32),
            pltpu.VMEM((4, 4, 128), F32),
            pltpu.VMEM((4, 128), F32),
            pltpu.VMEM((n_freq, 4, 128), F32),
            dma((7,)),
            dma((5,)),
            dma((4, 2)),
            dma((3,)),
            dma((4,)),
            dma((n_freq,)),
            dma((n_freq,)),
            dma((chunks,)),
            dma((chunks,)),
            dma((chunks,)),
            dma((chunks,)),
            dma((chunks,)),
            dma((4, chunks)),
            dma((2, chunks)),
            dma((4,)),
            dma((4,)),
            dma((n_freq,)),
            dma((n_freq,)),
        ],
        compiler_params=pltpu.CompilerParams(
            collective_id=0, has_side_effects=True, vmem_limit_bytes=60 * 2**20
        ),
        cost_estimate=pl.CostEstimate(flops=2 * 10**9, bytes_accessed=4 * 10**6, transcendentals=4096),
        name="migrate",
    )(slot_freq, traces, shot_of_trace, receiver_cell, slowness, image_model, operators)
    return gradient, tops


def solution(mesh):
    in_specs = (
        P("freq", None),
        P("freq", None),
        P("freq", None),
        P("freq"),
        P("depth", "freq", None, None, None),
        P("depth", None),
        P("depth", None),
    )
    out_specs = (P("depth", None), P("depth", "freq", None, None, None))
    return jax.shard_map(body, mesh=mesh, in_specs=in_specs, out_specs=out_specs, check_vma=False)
```

time: 105 us -> 98.9 us (0.942)
  local copies, waits for them, and re-layouts: 7.33 us -> 3.32 us
  Pallas kernels: 96.9 us -> 94.8 us
    unnamed x16 -> x2, local copies, waits for them, and re-layouts: 7.33 us -> 3.32 us
    pallas_call x1, Pallas kernels: 96.9 us -> 94.8 us  [body(): pl.pallas_call(functools.partial(kernel, n_depth, n_freq), out_shape=(jax...]
where the time goes in v2:
time: 98.9 us; the launch traced here: 98.7 us
  Pallas kernels  94.8 us (96%)
  local copies, waits for them, and re-layouts  3.32 us (3%)
    pallas_call x1, Pallas kernels, body(): pl.pallas_call(functools.partial(kernel, n_depth, n_freq), out_shape=(jax...  94.8 us
    unnamed x2, local copies, waits for them, and re-layouts  3.32 us

profile of v2, /device:TPU:1, one launch (start us, length us, event | category | flops | bytes accessed | tf_op | source)
XLA Modules:
  0.0 98.7 jit_solution(15696773431056049694)
XLA Ops:
  0.6 94.8 %migrate.1 = (f32[1,512]{1,0:T(1,128)}, bf16[1,2,2,192,512]{4,3,2,1,0:T(8,128)(2,1)}) custom-call(s32[2]{0:T(128)} %slot_hbm.1, bf16[512,128]{1,0:T(8,128)(2,1)} %traces_hbm.1, s32[1,512]{1,0:T(1,128)} %shot_hbm.1, s32[1,512]{1,0:T(1,128)} %cell_hbm.1, f32[1,512]{1,0:T(1,128)} %slow_hbm.1, f32[1,512]{1,0:T(1,128)} %model_hbm.1, ...), custom_call_target="tpu_custom_call" | custom-call | flops 2000000000 | bytes 4000000 | tf_op jit(solution)/shard_map/migrate/pallas_call | solution.py:676
  95.4 1.3 %copy.11 = f32[1,512]{1,0:T(1,128)} copy(f32[1,512]{1,0:T(1,128)} %get-tuple-element.4) | data formatting | bytes 4096
  96.7 2.1 %copy.12 = bf16[1,2,2,192,512]{4,3,2,1,0:T(8,128)(2,1)} copy(bf16[1,2,2,192,512]{4,3,2,1,0:T(8,128)(2,1)} %get-tuple-element.5) | data formatting | bytes 1572864

commit v3 on v2

--- a/solution.py
+++ b/solution.py
@@ -10,7 +10,7 @@
 MESH = pl.DeviceIdType.MESH
 SHOTS_DEV = 6
 SH = 32
-SINGLES = 4
+HALF = 2
 F32 = jnp.float32
 BF16 = jnp.bfloat16
 
@@ -88,34 +88,25 @@
     c = d % 2
     chunks = din.shape[0]
     lateral = din.shape[-1]
-    single = z < SINGLES
-    paired = z >= SINGLES
-    final = z >= n_depth // 2 - 2
-    side = z % 2
-    slot = jnp.where(single, c, side)
-    rank = jnp.where(single, c, 2 * side + c)
-    base = d - rank
-    mine = jnp.where(single, chunks, chunks // 2)
-    partner = base + jnp.where(single, 1 - c, 2 * side + 1 - c)
-    across = base + 2 * (1 - side) + c
-    across_other = base + 2 * (1 - side) + 1 - c
-    edge = 2 * SINGLES
+    last = n_depth // 2 - 1
+    odd = z % 2 == 1
+    host = odd & (z < last)
+    helper = jnp.logical_not(odd) & (z > 0)
+    base = 2 * z
+    partner = base + 1 - c
+    cross = jnp.where(host, d + 2, d - 2) + 1 - 2 * c
 
     def at(depth):
         return {"depth": depth}
 
-    def place_of(turn):
-        return jnp.where(single, turn, 2 * turn + c)
-
     first_chunk = (f * SHOTS_DEV) // SH
 
     def chunk_of(place):
         return (first_chunk + place) % chunks
 
-    def down_target(place):
-        return jnp.where(z < SINGLES - 1, d + 2, jnp.where(single, edge + 2 * c + place % 2, (d + 4) % n_depth))
-
-    up_target = jnp.where(single, (d + n_depth - 2) % n_depth, jnp.where(z < SINGLES + 2, edge - 2 + side, d - 4))
+    below = (d + 2) % n_depth
+    above = (d + n_depth - 2) % n_depth
+    up_target = jnp.where(z > 1, (d + n_depth - 4) % n_depth, above)
 
     barrier = pltpu.get_barrier_semaphore()
 
@@ -130,27 +121,31 @@
 
     @pl.when(z > 0)
     def _():
+        greet(above)
+
+    @pl.when(z < last)
+    def _():
+        greet(below)
+
+    @pl.when(host)
+    def _():
+        greet((d + 4) % n_depth)
+
+    @pl.when(odd & (z > 1))
+    def _():
         greet(up_target)
 
-    @pl.when(jnp.logical_not(final))
-    def _():
-        greet(down_target(0))
-
-    @pl.when(z == SINGLES - 1)
-    def _():
-        greet(down_target(1))
-
-    @pl.when(paired)
-    def _():
-        greet(across)
-        greet(across_other)
+    @pl.when(host | helper)
+    def _():
+        greet(cross)
 
     greeted = (
         n_freq
         + jnp.where(z > 0, 1, 0)
-        + jnp.where(final, 0, 1)
-        + jnp.where(z == SINGLES - 1, 1, 0)
-        + jnp.where(paired, 2, 0)
+        + jnp.where(z < last, 1, 0)
+        + jnp.where(host, 1, 0)
+        + jnp.where(odd & (z > 1), 1, 0)
+        + jnp.where(host | helper, 1, 0)
     )
 
     loads = [
@@ -163,7 +158,7 @@
                 (traces_hbm, traces_ref),
                 (shot_hbm, shot_ref),
                 (cell_hbm, cell_ref),
-                (oper_ref.at[0, slot], opn.at[rank]),
+                (oper_ref.at[0, c], opn.at[c]),
             ]
         )
     ]
@@ -179,7 +174,7 @@
         load.wait()
 
     row8 = lax.broadcasted_iota(jnp.int32, (8, lateral), 0)
-    par[rank] = jnp.where(row8 == 0, slow_ref[...], model_ref[...])
+    par[c] = jnp.where(row8 == 0, slow_ref[...], model_ref[...])
 
     @pl.when(z == 0)
     def _():
@@ -233,92 +228,65 @@
 
         box_copy(n_freq // 2).start()
 
-    def par_copy(mate, index, target):
+    def par_copy(index, place, send, target):
         return pltpu.make_async_remote_copy(
             src_ref=par.at[index],
-            dst_ref=par.at[index],
-            send_sem=par_send.at[mate],
-            recv_sem=par_recv.at[index],
+            dst_ref=par.at[place],
+            send_sem=par_send.at[send],
+            recv_sem=par_recv.at[place],
             device_id=at(target),
             device_id_type=MESH,
         )
 
-    def oper_copy(source, index, send, target):
+    def oper_copy(source, place, target):
         return pltpu.make_async_remote_copy(
             src_ref=source,
-            dst_ref=opn.at[index],
-            send_sem=oper_send.at[send],
-            recv_sem=oper_recv.at[index, 0],
+            dst_ref=opn.at[place],
+            send_sem=oper_send.at[place],
+            recv_sem=oper_recv.at[place],
             device_id=at(target),
             device_id_type=MESH,
         )
 
-    def half_copy(source, index, p, send, target):
-        return pltpu.make_async_remote_copy(
-            src_ref=source,
-            dst_ref=opn.at[index, p],
-            send_sem=oper_send.at[send],
-            recv_sem=oper_recv.at[index, p],
-            device_id=at(target),
-            device_id_type=MESH,
-        )
-
-    partner_rank = partner - base
-    across_rank = across - base
-    other_rank = across_other - base
-    to_partner = oper_copy(oper_ref.at[0, jnp.where(single, 1 - c, side)], rank, 0, partner)
-    from_partner = oper_copy(oper_ref.at[0, slot], partner_rank, 0, partner)
-
-    @pl.when(paired)
-    def _():
-        for p in range(2):
-            half_copy(oper_ref.at[0, 1 - side, p], rank, p, 1 + p, across).start()
-
-    par_copy(0, rank, partner).start()
+    to_partner = oper_copy(oper_ref.at[0, 1 - c], c, partner)
     to_partner.start()
-
-    @pl.when(paired)
-    def _():
-        par_copy(1, rank, across).start()
-        par_copy(2, rank, across_other).start()
+    par_copy(c, c, 0, partner).start()
+
+    @pl.when(helper)
+    def _():
+        par_copy(c, 2 + c, 1, above).start()
+        par_copy(c, 2 + c, 2, cross).start()
+
+    def lend(e):
+        return oper_copy(opn.at[e], 2 + e, above)
 
     loads[2].wait()
     loads[6].wait()
-    scale = 0.1 * (slot_ref[slot].astype(F32) + 1.0)
+    scale = 0.1 * (slot_ref[c].astype(F32) + 1.0)
 
     def angles(e):
         theta = scale * par[e, 0:1, :]
         cosines[e] = jnp.cos(theta)
         sines[e] = jnp.sin(theta)
 
+    @pl.when(helper & (z > 2))
+    def _():
+        lend(c).start()
+
     gacc[...] = jnp.zeros_like(gacc)
-
-    @pl.when(single)
-    def _():
-        for p in range(2):
-            opt[rank, p] = opn[rank, p].T
-
-    par_copy(0, partner_rank, partner).wait_recv()
-    angles(rank)
-    angles(partner_rank)
-    from_partner.wait_recv()
-
-    @pl.when(single)
-    def _():
-        for p in range(2):
-            opt[partner_rank, p] = opn[partner_rank, p].T
-
-    @pl.when(paired)
-    def _():
-        par_copy(1, across_rank, across).wait_recv()
-        par_copy(2, other_rank, across_other).wait_recv()
-        angles(across_rank)
-        angles(other_rank)
-        for p in range(2):
-            half_copy(oper_ref.at[0, slot, p], across_rank, p, 1 + p, across).wait_recv()
-            half_copy(opn.at[across_rank, p], across_rank, p, 3 + p, partner).start()
-        for p in range(2):
-            half_copy(opn.at[other_rank, p], other_rank, p, 3 + p, partner).wait_recv()
+    for p in range(2):
+        opt[c, p] = opn[c, p].T
+    par_copy(1 - c, 1 - c, 0, partner).wait_recv()
+    angles(0)
+    angles(1)
+    oper_copy(oper_ref.at[0, c], 1 - c, partner).wait_recv()
+
+    @pl.when(helper & (z > 2))
+    def _():
+        lend(1 - c).start()
+
+    for p in range(2):
+        opt[1 - c, p] = opn[1 - c, p].T
 
     def wait_box(source):
         @pl.when(source != f)
@@ -368,22 +336,26 @@
             for high in range(4):
                 din[place, p, :, 128 * high : 128 * (high + 1)] = bins[4 * p + high, 8 : 8 + SH, :].astype(BF16)
 
-    def down_copy(place):
+    def columns(half):
+        width = lateral // HALF
+        return pl.ds(half * width, width)
+
+    def down_copy(place, half):
         return pltpu.make_async_remote_copy(
-            src_ref=dout.at[place],
-            dst_ref=din.at[place],
-            send_sem=down_send.at[place],
-            recv_sem=down_recv.at[place],
-            device_id=at(down_target(place)),
-            device_id_type=MESH,
-        )
-
-    def up_copy(place):
+            src_ref=dout.at[place, :, :, columns(half)],
+            dst_ref=din.at[place, :, :, columns(half)],
+            send_sem=down_send.at[place, half],
+            recv_sem=down_recv.at[place, half],
+            device_id=at(below),
+            device_id_type=MESH,
+        )
+
+    def up_copy(place, half):
         return pltpu.make_async_remote_copy(
-            src_ref=abuf.at[0, place],
-            dst_ref=uin.at[place],
-            send_sem=up_send.at[place],
-            recv_sem=up_recv.at[place],
+            src_ref=abuf.at[0, place, :, :, columns(half)],
+            dst_ref=uin.at[place, :, :, columns(half)],
+            send_sem=up_send.at[place, half],
+            recv_sem=up_recv.at[place, half],
             device_id=at(up_target),
             device_id_type=MESH,
         )
@@ -399,41 +371,32 @@
     def forward(stacked, by_real, by_imag):
         return (by_real[:SH] - by_imag[SH:]).astype(BF16), (by_imag[:SH] + by_real[SH:]).astype(BF16)
 
-    def forward_single(e, stacked):
-        return forward(stacked, product(stacked, opt[e, 0]), product(stacked, opt[e, 1]))
-
-    def forward_pair(e, stacked):
-        return forward(stacked, product_rows(stacked, opn[e, 0]), product_rows(stacked, opn[e, 1]))
-
-    def send_down(place, real, imag):
-        dout[place, 0] = real
-        dout[place, 1] = imag
-        down_copy(place).start()
-
-    def down_single(place):
+    def down(place):
         stacked = shift(0, place, din[place, 0].astype(F32), din[place, 1].astype(F32))
-        real, imag = forward_single(0, stacked)
+        real, imag = forward(stacked, product(stacked, opt[0, 0]), product(stacked, opt[0, 1]))
         stacked = shift(1, place, real.astype(F32), imag.astype(F32))
-        real, imag = forward_single(1, stacked)
-        send_down(place, real, imag)
-
-    def down_pair(place):
-        real, imag = din[place, 0], din[place, 1]
-        for e in range(3):
-            stacked = shift(e, place, real.astype(F32), imag.astype(F32))
-            real, imag = forward_pair(e, stacked)
-        stacked = shift(3, place, real.astype(F32), imag.astype(F32))
-
-        @pl.when(jnp.logical_not(final))
+
+        @pl.when(z < last)
         def _():
-            real, imag = forward_pair(3, stacked)
-            send_down(place, real, imag)
+            for half in range(HALF):
+                cols = columns(half)
+                real, imag = forward(
+                    stacked, product(stacked, opt[1, 0, :, cols]), product(stacked, opt[1, 1, :, cols])
+                )
+                dout[place, 0, :, cols] = real
+                dout[place, 1, :, cols] = imag
+                down_copy(place, half).start()
+
+    def again(place):
+        stacked = shift(2, place, dout[place, 0].astype(F32), dout[place, 1].astype(F32))
+        real, imag = forward(stacked, product_rows(stacked, opn[2, 0]), product_rows(stacked, opn[2, 1]))
+        shift(3, place, real.astype(F32), imag.astype(F32))
 
     def rows_of(place):
         return pl.ds(pl.multiple_of(chunk_of(place) * SH, SH), SH)
 
     def tops_here(e, place):
-        return pltpu.make_async_copy(abuf.at[e, place], tops_ref.at[0, slot, :, rows_of(place), :], tops_local.at[place])
+        return pltpu.make_async_copy(abuf.at[e, place], tops_ref.at[0, c, :, rows_of(place), :], tops_local.at[place])
 
     def tops_there(e, place, its_slot):
         return pltpu.make_async_remote_copy(
@@ -453,79 +416,98 @@
         term = old_real * source_real + old_imag * source_imag
         gacc[e] += jnp.sum(term.reshape(SH // 8, 8, lateral), axis=0)
         stacked = jnp.concatenate([source_real.astype(BF16), source_imag.astype(BF16)], axis=0)
-        by_real = product(stacked, opn[e, 0])
-        by_imag = product(stacked, opn[e, 1])
-        back_real = by_real[:SH] + by_imag[SH:]
-        back_imag = by_real[SH:] - by_imag[:SH]
-        cos_row, sin_row = cosines[e], sines[e]
-        out_real = (cos_row * back_real + sin_row * back_imag).astype(BF16)
-        out_imag = (cos_row * back_imag - sin_row * back_real).astype(BF16)
-        abuf[e, place, 0] = out_real
-        abuf[e, place, 1] = out_imag
-
-        if e == 0:
-
-            @pl.when(z > 0)
+        pieces = HALF if e == 0 else 1
+        width = lateral // pieces
+        result = []
+        for piece in range(pieces):
+            cols = pl.ds(piece * width, width)
+            by_real = product(stacked, opn[e, 0, :, cols])
+            by_imag = product(stacked, opn[e, 1, :, cols])
+            back_real = by_real[:SH] + by_imag[SH:]
+            back_imag = by_real[SH:] - by_imag[:SH]
+            cos_row, sin_row = cosines[e, :, cols], sines[e, :, cols]
+            out_real = (cos_row * back_real + sin_row * back_imag).astype(BF16)
+            out_imag = (cos_row * back_imag - sin_row * back_real).astype(BF16)
+            abuf[e, place, 0, :, cols] = out_real
+            abuf[e, place, 1, :, cols] = out_imag
+            result = out_real.astype(F32), out_imag.astype(F32)
+            if e == 0:
+
+                @pl.when(z > 0)
+                def _():
+                    up_copy(place, piece).start()
+
+        if e < 2:
+
+            @pl.when(c == e)
             def _():
-                up_copy(place).start()
-
-        @pl.when(rank == e)
-        def _():
-            tops_here(e, place).start()
-
-        @pl.when(rank != e)
-        def _():
-            tops_there(e, place, slot).start()
-
-        return out_real.astype(F32), out_imag.astype(F32)
+                tops_here(e, place).start()
+
+            @pl.when(c != e)
+            def _():
+                tops_there(e, place, c).start()
+
+        else:
+            tops_there(e, place, c).start()
+        return result
 
     def up(place, steps):
         real, imag = uin[place, 0].astype(F32), uin[place, 1].astype(F32)
         for e in reversed(range(steps)):
             real, imag = backward(e, place, real, imag)
 
-    @pl.when(single)
+    @pl.when(z == last)
+    def _():
+        uin[...] = jnp.zeros_like(uin)
+
+    @pl.loop(0, chunks)
+    def _(place):
+        @pl.when(z == 0)
+        def _():
+            bin_chunk(place)
+
+        @pl.when(z > 0)
+        def _():
+            for half in range(HALF):
+                down_copy(place, half).wait_recv()
+
+        down(place)
+
+        @pl.when(z == last)
+        def _():
+            up(place, 2)
+
+    @pl.when(z == 2)
+    def _():
+        lend(0).start()
+        lend(1).start()
+
+    def wait_up(place):
+        for half in range(HALF):
+            up_copy(place, half).wait_recv()
+
+    @pl.when(z == 0)
     def _():
         @pl.loop(0, chunks)
         def _(place):
-            @pl.when(z == 0)
-            def _():
-                bin_chunk(place)
-
-            @pl.when(z > 0)
-            def _():
-                down_copy(place).wait_recv()
-
-            down_single(place)
+            wait_up(place)
+            up(place, 2)
+
+    @pl.when(host)
+    def _():
+        for e in range(2, 4):
+            par_copy(e, e, 0, partner).wait_recv()
+            angles(e)
+            oper_copy(opn.at[e], e, partner).wait_recv()
 
         @pl.loop(0, chunks)
         def _(place):
-            up_copy(place).wait_recv()
-            up(place, 2)
-
-    @pl.when(final)
-    def _():
-        uin[...] = jnp.zeros_like(uin)
-
-    @pl.when(paired)
-    def _():
-        @pl.loop(0, 2 * mine)
-        def _(turn):
-            going_down = jnp.where(final, turn % 2 == 0, turn < mine)
-            place = place_of(jnp.where(final, turn // 2, turn % mine))
-
-            @pl.when(going_down)
-            def _():
-                down_copy(place).wait_recv()
-                down_pair(place)
-
-            @pl.when(jnp.logical_not(going_down))
-            def _():
-                @pl.when(jnp.logical_not(final))
-                def _():
-                    up_copy(place).wait_recv()
-
-                up(place, 4)
+            again(place)
+
+        @pl.loop(0, chunks)
+        def _(place):
+            wait_up(place)
+            up(place, 4)
 
     row4 = lax.broadcasted_iota(jnp.int32, (4, 128), 0)
 
@@ -548,34 +530,34 @@
     def share(steps):
         for e in range(steps):
             gpart[e] = rows_tile(jnp.sum(gacc[e], axis=0, keepdims=True))
-
-            @pl.when(rank != e)
-            def _():
-                part_copy(e, rank).start()
-
-        total = gpart[rank]
-        for e in range(steps):
-
-            @pl.when(rank != e)
-            def _():
-                part_copy(e, e).wait_recv()
-
-            @pl.when(rank == e)
-            def _():
-                gin[e] = jnp.zeros((4, 128), F32)
-
-        for e in range(steps):
-            total = total + gin[e]
-        gsend[...] = total
-        gbox[f] = total
-
-    @pl.when(single)
+            if e < 2:
+
+                @pl.when(c != e)
+                def _():
+                    part_copy(e, c).start()
+
+            else:
+                part_copy(e, c).start()
+
+        part_copy(0, 1 - c).wait_recv()
+        gin[c] = gpart[c]
+
+    @pl.when(host)
+    def _():
+        share(4)
+
+    @pl.when((z == 0) | (z == last))
     def _():
         share(2)
 
-    @pl.when(paired)
-    def _():
-        share(4)
+    @pl.when(helper)
+    def _():
+        part_copy(0, 0).wait_recv()
+        part_copy(0, 1).wait_recv()
+
+    total = gin[0] + gin[1]
+    gsend[...] = total
+    gbox[f] = total
 
     def g_copy(k):
         return pltpu.make_async_remote_copy(
@@ -607,15 +589,14 @@
     grad_ref[...] = jnp.concatenate([total[q : q + 1] for q in range(4)], axis=1)
 
     to_partner.wait_send()
-    par_copy(0, rank, partner).wait_send()
-
-    @pl.when(paired)
-    def _():
-        par_copy(1, rank, across).wait_send()
-        par_copy(2, rank, across_other).wait_send()
-        for p in range(2):
-            half_copy(oper_ref.at[0, 1 - side, p], rank, p, 1 + p, across).wait_send()
-            half_copy(opn.at[across_rank, p], across_rank, p, 3 + p, partner).wait_send()
+    par_copy(c, c, 0, partner).wait_send()
+
+    @pl.when(helper)
+    def _():
+        par_copy(c, 2 + c, 1, above).wait_send()
+        par_copy(c, 2 + c, 2, cross).wait_send()
+        lend(0).wait_send()
+        lend(1).wait_send()
 
     @pl.loop(1, n_freq)
     def _(k):
@@ -627,40 +608,39 @@
         def _(k):
             box_copy(k).wait_send()
 
-    steps = jnp.where(single, 2, 4)
+    steps = jnp.where(host, 4, jnp.where(helper, 0, 2))
 
     @pl.loop(0, steps)
     def _(e):
-        @pl.when(rank != e)
+        @pl.when(c != e)
         def _():
-            part_copy(e, rank).wait_send()
-
-            @pl.loop(0, mine)
-            def _(turn):
-                tops_there(e, place_of(turn), slot).wait_send()
-
-    @pl.loop(0, mine)
-    def _(turn):
-        place = place_of(turn)
-
-        @pl.when(jnp.logical_not(final))
+            part_copy(e, c).wait_send()
+
+            @pl.loop(0, chunks)
+            def _(place):
+                tops_there(e, place, c).wait_send()
+
+    @pl.loop(0, chunks)
+    def _(place):
+        for half in range(HALF):
+
+            @pl.when(z < last)
+            def _():
+                down_copy(place, half).wait_send()
+
+            @pl.when((z > 0) & jnp.logical_not(helper))
+            def _():
+                up_copy(place, half).wait_send()
+
+        tops_there(0, place, 1 - c).wait_recv()
+
+        @pl.when(helper)
         def _():
-            down_copy(place).wait_send()
-
-        @pl.when(z > 0)
+            tops_there(0, place, c).wait_recv()
+
+        @pl.when(jnp.logical_not(helper))
         def _():
-            up_copy(place).wait_send()
-
-        tops_here(rank, place).wait()
-
-    @pl.loop(0, 2 * chunks)
-    def _(index):
-        its_slot, place = index // chunks, index % chunks
-        sender = jnp.where(single, its_slot, 2 * its_slot + place % 2)
-
-        @pl.when(sender != rank)
-        def _():
-            tops_there(rank, place, its_slot).wait_recv()
+            tops_here(c, place).wait()
 
 
 def body(traces, shot_of_trace, receiver_cell, slot_freq, operators, slowness, image_model):
@@ -703,25 +683,25 @@
             pltpu.VMEM((4, chunks) + block, BF16),
             pltpu.VMEM((4, 8, lateral), F32),
             pltpu.VMEM((4, 4, 128), F32),
-            pltpu.VMEM((4, 4, 128), F32),
+            pltpu.VMEM((2, 4, 128), F32),
             pltpu.VMEM((4, 128), F32),
             pltpu.VMEM((n_freq, 4, 128), F32),
             dma((7,)),
-            dma((5,)),
-            dma((4, 2)),
+            dma((4,)),
+            dma((4,)),
             dma((3,)),
             dma((4,)),
             dma((n_freq,)),
             dma((n_freq,)),
-            dma((chunks,)),
-            dma((chunks,)),
-            dma((chunks,)),
-            dma((chunks,)),
+            dma((chunks, HALF)),
+            dma((chunks, HALF)),
+            dma((chunks, HALF)),
+            dma((chunks, HALF)),
             dma((chunks,)),
             dma((4, chunks)),
             dma((2, chunks)),
             dma((4,)),
-            dma((4,)),
+            dma((2,)),
             dma((n_freq,)),
             dma((n_freq,)),
         ],

time: 98.9 us -> 111 us (1.12)
  Pallas kernels: 94.8 us -> 107 us
    pallas_call x1, Pallas kernels: 94.8 us -> 107 us  [body(): pl.pallas_call(functools.partial(kernel, n_depth, n_freq), out_shape=(jax...]
where the time goes in v3:
time: 111 us
  Pallas kernels  107 us (96%)
  local copies, waits for them, and re-layouts  3.32 us (3%)
    pallas_call x1, Pallas kernels, body(): pl.pallas_call(functools.partial(kernel, n_depth, n_freq), out_shape=(jax...  107 us
    unnamed x2, local copies, waits for them, and re-layouts  3.32 us

profile of v3, /device:TPU:1, one launch (start us, length us, event | category | flops | bytes accessed | tf_op | source)
XLA Modules:
  0.0 110.9 jit_solution(5839060913029996439)
XLA Ops:
  0.6 106.9 %migrate.1 = (f32[1,512]{1,0:T(1,128)}, bf16[1,2,2,192,512]{4,3,2,1,0:T(8,128)(2,1)}) custom-call(s32[2]{0:T(128)} %slot_hbm.1, bf16[512,128]{1,0:T(8,128)(2,1)} %traces_hbm.1, s32[1,512]{1,0:T(1,128)} %shot_hbm.1, s32[1,512]{1,0:T(1,128)} %cell_hbm.1, f32[1,512]{1,0:T(1,128)} %slow_hbm.1, f32[1,512]{1,0:T(1,128)} %model_hbm.1, ...), custom_call_target="tpu_custom_call" | custom-call | flops 2000000000 | bytes 4000000 | tf_op jit(solution)/shard_map/migrate/pallas_call | solution.py:656
  107.6 1.3 %copy.11 = f32[1,512]{1,0:T(1,128)} copy(f32[1,512]{1,0:T(1,128)} %get-tuple-element.4) | data formatting | bytes 4096
  108.8 2.1 %copy.12 = bf16[1,2,2,192,512]{4,3,2,1,0:T(8,128)(2,1)} copy(bf16[1,2,2,192,512]{4,3,2,1,0:T(8,128)(2,1)} %get-tuple-element.5) | data formatting | bytes 1572864

commit v4 on v3

--- a/solution.py
+++ b/solution.py
@@ -9,8 +9,10 @@
 
 MESH = pl.DeviceIdType.MESH
 SHOTS_DEV = 6
-SH = 32
-HALF = 2
+SH = 16
+HALF = 1
+HOSTS = ()
+EARLY = ()
 F32 = jnp.float32
 BF16 = jnp.bfloat16
 
@@ -89,9 +91,17 @@
     chunks = din.shape[0]
     lateral = din.shape[-1]
     last = n_depth // 2 - 1
-    odd = z % 2 == 1
-    host = odd & (z < last)
-    helper = jnp.logical_not(odd) & (z > 0)
+
+    def among(chips, shift=0):
+        found = z < 0
+        for chip in chips:
+            found = found | (z == chip + shift)
+        return found
+
+    host = among(HOSTS)
+    helper = among(HOSTS, 1)
+    early = among(EARLY, 1)
+    skips = among(HOSTS, 2)
     base = 2 * z
     partner = base + 1 - c
     cross = jnp.where(host, d + 2, d - 2) + 1 - 2 * c
@@ -106,7 +116,7 @@
 
     below = (d + 2) % n_depth
     above = (d + n_depth - 2) % n_depth
-    up_target = jnp.where(z > 1, (d + n_depth - 4) % n_depth, above)
+    up_target = jnp.where(skips, (d + n_depth - 4) % n_depth, above)
 
     barrier = pltpu.get_barrier_semaphore()
 
@@ -131,7 +141,7 @@
     def _():
         greet((d + 4) % n_depth)
 
-    @pl.when(odd & (z > 1))
+    @pl.when(skips)
     def _():
         greet(up_target)
 
@@ -144,7 +154,7 @@
         + jnp.where(z > 0, 1, 0)
         + jnp.where(z < last, 1, 0)
         + jnp.where(host, 1, 0)
-        + jnp.where(odd & (z > 1), 1, 0)
+        + jnp.where(skips, 1, 0)
         + jnp.where(host | helper, 1, 0)
     )
 
@@ -269,7 +279,7 @@
         cosines[e] = jnp.cos(theta)
         sines[e] = jnp.sin(theta)
 
-    @pl.when(helper & (z > 2))
+    @pl.when(early)
     def _():
         lend(c).start()
 
@@ -281,7 +291,7 @@
     angles(1)
     oper_copy(oper_ref.at[0, c], 1 - c, partner).wait_recv()
 
-    @pl.when(helper & (z > 2))
+    @pl.when(early)
     def _():
         lend(1 - c).start()
 
@@ -300,7 +310,8 @@
                 device_id_type=MESH,
             ).wait_recv()
 
-    sources = max((SH * j + SH - 1) // SHOTS_DEV - SH * j // SHOTS_DEV + 1 for j in range(chunks))
+    counts = [(SH * j + SH - 1) // SHOTS_DEV - SH * j // SHOTS_DEV + 1 for j in range(chunks)]
+    fewest, most = min(counts), max(counts)
 
     def bin_chunk(place):
         j = chunk_of(place)
@@ -320,7 +331,8 @@
         top = 8 + SHOTS_DEV * first_source - start
         row = lax.broadcasted_iota(jnp.int32, (32, 4 * 128), 0).astype(F32)
         lane_row = lax.broadcasted_iota(jnp.int32, (128, 4 * 128), 0).astype(F32)
-        for i in range(sources):
+
+        def add_source(i):
             tile = inbox[first_source + i].astype(F32)
             real, imag = lanes(tile, 0, 512), lanes(tile, 1, 512)
             first, low = lanes(tile, 2, 512), lanes(tile, 3, 512)
@@ -332,6 +344,16 @@
             part = lax.dot_general(left, right, (((1,), (1,)), ((), ())), preferred_element_type=F32)
             for g in range(8):
                 bins[g, pl.ds(top + SHOTS_DEV * i, 8), :] = part[8 * g : 8 * (g + 1)]
+
+        for i in range(fewest):
+            add_source(i)
+
+        for i in range(fewest, most):
+
+            @pl.when(first_source + i <= (start + SH - 1) // SHOTS_DEV)
+            def _():
+                add_source(i)
+
         for p in range(2):
             for high in range(4):
                 din[place, p, :, 128 * high : 128 * (high + 1)] = bins[4 * p + high, 8 : 8 + SH, :].astype(BF16)
@@ -477,7 +499,7 @@
         def _():
             up(place, 2)
 
-    @pl.when(z == 2)
+    @pl.when(helper & jnp.logical_not(early))
     def _():
         lend(0).start()
         lend(1).start()
@@ -486,7 +508,9 @@
         for half in range(HALF):
             up_copy(place, half).wait_recv()
 
-    @pl.when(z == 0)
+    plain = jnp.logical_not(host | helper)
+
+    @pl.when(plain & (z < last))
     def _():
         @pl.loop(0, chunks)
         def _(place):
@@ -546,7 +570,7 @@
     def _():
         share(4)
 
-    @pl.when((z == 0) | (z == last))
+    @pl.when(plain)
     def _():
         share(2)
 

time: 111 us -> 91.8 us (0.83)
  Pallas kernels: 107 us -> 87.7 us
    pallas_call x1, Pallas kernels: 107 us -> 87.7 us  [body(): pl.pallas_call(functools.partial(kernel, n_depth, n_freq), out_shape=(jax...]
where the time goes in v4:
time: 91.8 us; the launch traced here: 91.6 us
  Pallas kernels  87.7 us (96%)
  local copies, waits for them, and re-layouts  3.32 us (4%)
    pallas_call x1, Pallas kernels, body(): pl.pallas_call(functools.partial(kernel, n_depth, n_freq), out_shape=(jax...  87.7 us
    unnamed x2, local copies, waits for them, and re-layouts  3.32 us

profile of v4, /device:TPU:1, one launch (start us, length us, event | category | flops | bytes accessed | tf_op | source)
XLA Modules:
  0.0 91.6 jit_solution(16066762767460902732)
XLA Ops:
  0.6 87.7 %migrate.1 = (f32[1,512]{1,0:T(1,128)}, bf16[1,2,2,192,512]{4,3,2,1,0:T(8,128)(2,1)}) custom-call(s32[2]{0:T(128)} %slot_hbm.1, bf16[512,128]{1,0:T(8,128)(2,1)} %traces_hbm.1, s32[1,512]{1,0:T(1,128)} %shot_hbm.1, s32[1,512]{1,0:T(1,128)} %cell_hbm.1, f32[1,512]{1,0:T(1,128)} %slow_hbm.1, f32[1,512]{1,0:T(1,128)} %model_hbm.1, ...), custom_call_target="tpu_custom_call" | custom-call | flops 2000000000 | bytes 4000000 | tf_op jit(solution)/shard_map/migrate/pallas_call | solution.py:680
  88.3 1.3 %copy.11 = f32[1,512]{1,0:T(1,128)} copy(f32[1,512]{1,0:T(1,128)} %get-tuple-element.4) | data formatting | bytes 4096
  89.6 2.1 %copy.12 = bf16[1,2,2,192,512]{4,3,2,1,0:T(8,128)(2,1)} copy(bf16[1,2,2,192,512]{4,3,2,1,0:T(8,128)(2,1)} %get-tuple-element.5) | data formatting | bytes 1572864

commit v5 on v4

v5 whole, which is shorter than its diff:
```python
import functools

import jax
import jax.numpy as jnp
from jax import lax
from jax.experimental import pallas as pl
from jax.experimental.pallas import tpu as pltpu
from jax.sharding import PartitionSpec as P

MESH = pl.DeviceIdType.MESH
SHOTS_DEV = 6
SH = 16
F32 = jnp.float32
BF16 = jnp.bfloat16


def product(rows, matrix):
    return jnp.dot(rows, matrix, preferred_element_type=F32)


def lanes(tile, row, width):
    return jnp.concatenate([tile[4 * q + row : 4 * q + row + 1] for q in range(width // 128)], axis=1)


def kernel(
    n_depth,
    n_freq,
    slot_hbm,
    traces_hbm,
    shot_hbm,
    cell_hbm,
    slow_hbm,
    model_hbm,
    oper_ref,
    grad_ref,
    tops_ref,
    slot_ref,
    traces_ref,
    shot_ref,
    cell_ref,
    slow_ref,
    model_ref,
    opn,
    opt,
    par,
    cosines,
    sines,
    outbox,
    inbox,
    bins,
    din,
    dout,
    vbuf,
    uin,
    abuf,
    gacc,
    gpart,
    gin,
    gsend,
    gbox,
    load_sem,
    oper_send,
    oper_recv,
    par_send,
    par_recv,
    box_send,
    box_recv,
    down_send,
    down_recv,
    up_send,
    up_recv,
    tops_local,
    tops_send,
    tops_recv,
    part_send,
    part_recv,
    g_send,
    g_recv,
):
    d = lax.axis_index("depth")
    f = lax.axis_index("freq")
    z = d // 2
    c = d % 2
    chunks = din.shape[0]
    lateral = din.shape[-1]
    last = n_depth // 2 - 1
    base = 2 * z
    partner = base + 1 - c

    def at(depth):
        return {"depth": depth}

    first_chunk = (f * SHOTS_DEV) // SH

    def chunk_of(place):
        return (first_chunk + place) % chunks

    below = (d + 2) % n_depth
    above = (d + n_depth - 2) % n_depth

    barrier = pltpu.get_barrier_semaphore()

    def greet(depth):
        pl.semaphore_signal(barrier, inc=1, device_id=at(depth), device_id_type=MESH)

    def greet_group(k):
        pl.semaphore_signal(barrier, inc=1, device_id={"freq": (f + k) % n_freq}, device_id_type=MESH)

    greet_group(n_freq // 2)

    @pl.loop(1, n_freq // 2)
    def _(k):
        greet_group(n_freq // 2 + k)
        greet_group(n_freq // 2 - k)

    greet(partner)

    @pl.when(z > 0)
    def _():
        greet(above)

    @pl.when(z < last)
    def _():
        greet(below)

    greeted = n_freq + jnp.where(z > 0, 1, 0) + jnp.where(z < last, 1, 0)

    loads = [
        pltpu.make_async_copy(source, target, load_sem.at[i])
        for i, (source, target) in enumerate(
            [
                (slow_hbm, slow_ref),
                (model_hbm, model_ref),
                (slot_hbm, slot_ref),
                (traces_hbm, traces_ref),
                (shot_hbm, shot_ref),
                (cell_hbm, cell_ref),
                (oper_ref.at[0, c], opn.at[c]),
            ]
        )
    ]

    @pl.when(z == 0)
    def _():
        for load in loads[3:6]:
            load.start()

    for load in loads[:3] + loads[6:]:
        load.start()
    for load in loads[:2]:
        load.wait()

    row8 = lax.broadcasted_iota(jnp.int32, (8, lateral), 0)
    par[c] = jnp.where(row8 == 0, slow_ref[...], model_ref[...])

    @pl.when(z == 0)
    def _():
        for load in loads[3:6]:
            load.wait()
        rows = n_freq * 16
        row = lax.broadcasted_iota(jnp.int32, (rows, 128), 0)
        column = lax.broadcasted_iota(jnp.int32, (rows, 128), 1)
        group, within = row // 16, row % 16
        kind, piece = within % 4, within // 4
        wanted = jnp.where(kind < 2, group * 4 + 2 * c + kind, -1)
        total = jnp.zeros((rows, 128), F32)
        for q in range(4):
            select = jnp.where((column == wanted) & (piece == q), 1.0, 0.0).astype(BF16)
            total += lax.dot_general(
                select,
                traces_ref[128 * q : 128 * (q + 1), :],
                (((1,), (1,)), ((), ())),
                preferred_element_type=F32,
            )
        cell = cell_ref[...]
        first = (cell // 128 * 8 + shot_ref[...]).astype(F32)
        second = (cell % 128).astype(F32)
        row16 = lax.broadcasted_iota(jnp.int32, (16, 128), 0)
        label = jnp.zeros((16, 128), F32)
        for q in range(4):
            label = jnp.where(row16 == 4 * q + 2, first[:, 128 * q : 128 * (q + 1)], label)
            label = jnp.where(row16 == 4 * q + 3, second[:, 128 * q : 128 * (q + 1)], label)
        filled = total.reshape(n_freq, 16, 128) + label[None]
        outbox[...] = filled.astype(BF16)
        inbox[f] = outbox[f]

    pl.semaphore_wait(barrier, greeted)

    def box_copy(k):
        return pltpu.make_async_remote_copy(
            src_ref=outbox.at[(f + k) % n_freq],
            dst_ref=inbox.at[f],
            send_sem=box_send.at[k],
            recv_sem=box_recv.at[f],
            device_id={"freq": (f + k) % n_freq},
            device_id_type=MESH,
        )

    @pl.when(z == 0)
    def _():
        @pl.loop(1, n_freq // 2)
        def _(k):
            box_copy(k).start()
            box_copy(n_freq - k).start()

        box_copy(n_freq // 2).start()

    def par_copy(index):
        return pltpu.make_async_remote_copy(
            src_ref=par.at[index],
            dst_ref=par.at[index],
            send_sem=par_send,
            recv_sem=par_recv,
            device_id=at(partner),
            device_id_type=MESH,
        )

    def oper_copy(slot, index):
        return pltpu.make_async_remote_copy(
            src_ref=oper_ref.at[0, slot],
            dst_ref=opn.at[index],
            send_sem=oper_send,
            recv_sem=oper_recv,
            device_id=at(partner),
            device_id_type=MESH,
        )

    oper_copy(1 - c, c).start()
    par_copy(c).start()

    loads[2].wait()
    loads[6].wait()
    scale = 0.1 * (slot_ref[c].astype(F32) + 1.0)

    def angles(e):
        theta = scale * par[e, 0:1, :]
        cosines[e] = jnp.cos(theta)
        sines[e] = jnp.sin(theta)

    gacc[...] = jnp.zeros_like(gacc)
    for p in range(2):
        opt[c, p] = opn[c, p].T
    par_copy(1 - c).wait_recv()
    angles(0)
    angles(1)
    oper_copy(c, 1 - c).wait_recv()

    for p in range(2):
        opt[1 - c, p] = opn[1 - c, p].T

    def wait_box(source):
        @pl.when(source != f)
        def _():
            pltpu.make_async_remote_copy(
                src_ref=outbox.at[source],
                dst_ref=inbox.at[source],
                send_sem=box_send.at[source],
                recv_sem=box_recv.at[source],
                device_id={"freq": source},
                device_id_type=MESH,
            ).wait_recv()

    counts = [(SH * j + SH - 1) // SHOTS_DEV - SH * j // SHOTS_DEV + 1 for j in range(chunks)]
    fewest, most = min(counts), max(counts)

    def bin_chunk(place):
        j = chunk_of(place)
        start = SH * j
        first_source = start // SHOTS_DEV
        fresh = jnp.where(place == 0, first_source, (start + SHOTS_DEV - 1) // SHOTS_DEV)
        after = jnp.where(
            (place == chunks - 1) & (first_chunk > 0),
            (SH * first_chunk) // SHOTS_DEV,
            (start + SH - 1) // SHOTS_DEV + 1,
        )

        @pl.loop(fresh, after)
        def _(source):
            wait_box(source)

        top = 8 + SHOTS_DEV * first_source - start
        row = lax.broadcasted_iota(jnp.int32, (32, 4 * 128), 0).astype(F32)
        lane_row = lax.broadcasted_iota(jnp.int32, (128, 4 * 128), 0).astype(F32)

        def add_source(i):
            tile = inbox[first_source + i].astype(F32)
            real, imag = lanes(tile, 0, 512), lanes(tile, 1, 512)
            first, low = lanes(tile, 2, 512), lanes(tile, 3, 512)
            hit = row == first
            left = jnp.concatenate(
                [jnp.where(hit, real, 0.0).astype(BF16), jnp.where(hit, imag, 0.0).astype(BF16)], axis=0
            )
            right = jnp.where(lane_row == low, 1.0, 0.0).astype(BF16)
            part = lax.dot_general(left, right, (((1,), (1,)), ((), ())), preferred_element_type=F32)
            for g in range(8):
                bins[g, pl.ds(top + SHOTS_DEV * i, 8), :] = part[8 * g : 8 * (g + 1)]

        for i in range(fewest):
            add_source(i)

        for i in range(fewest, most):

            @pl.when(first_source + i <= (start + SH - 1) // SHOTS_DEV)
            def _():
                add_source(i)

        for p in range(2):
            for high in range(4):
                din[place, p, :, 128 * high : 128 * (high + 1)] = bins[4 * p + high, 8 : 8 + SH, :].astype(BF16)

    def down_copy(place):
        return pltpu.make_async_remote_copy(
            src_ref=dout.at[place],
            dst_ref=din.at[place],
            send_sem=down_send.at[place],
            recv_sem=down_recv.at[place],
            device_id=at(below),
            device_id_type=MESH,
        )

    def up_copy(place):
        return pltpu.make_async_remote_copy(
            src_ref=abuf.at[0, place],
            dst_ref=uin.at[place],
            send_sem=up_send.at[place],
            recv_sem=up_recv.at[place],
            device_id=at(above),
            device_id_type=MESH,
        )

    def load(ref, place, n):
        return [ref[pl.ds(place, n), p].reshape(n * SH, lateral).astype(F32) for p in range(2)]

    def store(ref, place, n, real, imag):
        ref[pl.ds(place, n), 0] = real.reshape(n, SH, lateral)
        ref[pl.ds(place, n), 1] = imag.reshape(n, SH, lateral)

    def shift(e, place, n, real, imag):
        cos_row, sin_row = cosines[e], sines[e]
        shifted_real = (cos_row * real - sin_row * imag).astype(BF16)
        shifted_imag = (cos_row * imag + sin_row * real).astype(BF16)
        store(vbuf.at[e], place, n, shifted_real, shifted_imag)
        return jnp.concatenate([shifted_real, shifted_imag], axis=0)

    def forward(e, stacked):
        rows = stacked.shape[0] // 2
        by_real, by_imag = product(stacked, opt[e, 0]), product(stacked, opt[e, 1])
        return (by_real[:rows] - by_imag[rows:]).astype(BF16), (by_imag[:rows] + by_real[rows:]).astype(BF16)

    def down(place, n, send):
        stacked = shift(0, place, n, *load(din, place, n))
        real, imag = forward(0, stacked)
        stacked = shift(1, place, n, real.astype(F32), imag.astype(F32))
        if send:
            real, imag = forward(1, stacked)
            store(dout, place, n, real, imag)
            for i in range(n):
                down_copy(place + i).start()

    def rows_of(place):
        return pl.ds(pl.multiple_of(chunk_of(place) * SH, SH), SH)

    def tops_here(e, place):
        return pltpu.make_async_copy(abuf.at[e, place], tops_ref.at[0, c, :, rows_of(place), :], tops_local.at[place])

    def tops_there(e, place, its_slot):
        return pltpu.make_async_remote_copy(
            src_ref=abuf.at[e, place],
            dst_ref=tops_ref.at[0, its_slot, :, rows_of(place), :],
            send_sem=tops_send.at[place],
            recv_sem=tops_recv.at[place],
            device_id=at(partner),
            device_id_type=MESH,
        )

    def backward(e, place, n, real, imag):
        rows = n * SH
        old_real, old_imag = load(vbuf.at[e], place, n)
        model = par[e, 1:2, :]
        source_real = real + model * old_real
        source_imag = imag + model * old_imag
        term = old_real * source_real + old_imag * source_imag
        gacc[e] += jnp.sum(term.reshape(rows // 8, 8, lateral), axis=0)
        stacked = jnp.concatenate([source_real.astype(BF16), source_imag.astype(BF16)], axis=0)
        by_real = product(stacked, opn[e, 0])
        by_imag = product(stacked, opn[e, 1])
        back_real = by_real[:rows] + by_imag[rows:]
        back_imag = by_real[rows:] - by_imag[:rows]
        cos_row, sin_row = cosines[e], sines[e]
        out_real = (cos_row * back_real + sin_row * back_imag).astype(BF16)
        out_imag = (cos_row * back_imag - sin_row * back_real).astype(BF16)
        store(abuf.at[e], place, n, out_real, out_imag)
        for i in range(n):
            if e == 0:

                @pl.when(z > 0)
                def _():
                    up_copy(place + i).start()

            @pl.when(c == e)
            def _():
                tops_here(e, place + i).start()

            @pl.when(c != e)
            def _():
                tops_there(e, place + i, c).start()

        return out_real.astype(F32), out_imag.astype(F32)

    def up(place, n, real, imag):
        real, imag = backward(1, place, n, real, imag)
        backward(0, place, n, real, imag)

    @pl.when(z == 0)
    def _():
        bin_chunk(0)
        down(0, 1, True)

        @pl.loop(0, (chunks - 2) // 2)
        def _(turn):
            place = 1 + 2 * turn
            bin_chunk(place)
            bin_chunk(place + 1)
            down(place, 2, True)

        bin_chunk(chunks - 1)
        down(chunks - 1, 1, True)

    @pl.when((z > 0) & (z < last))
    def _():
        @pl.loop(0, chunks)
        def _(place):
            down_copy(place).wait_recv()
            down(place, 1, True)

    @pl.when(z == last)
    def _():
        def turn_round(place, n):
            for i in range(n):
                down_copy(place + i).wait_recv()
            down(place, n, False)
            nothing = jnp.zeros((n * SH, lateral), F32)
            up(place, n, nothing, nothing)

        @pl.loop(0, (chunks - 2) // 2)
        def _(turn):
            turn_round(2 * turn, 2)

        @pl.loop(chunks - 2, chunks)
        def _(place):
            turn_round(place, 1)

    @pl.when(z < last)
    def _():
        @pl.loop(0, chunks)
        def _(place):
            up_copy(place).wait_recv()
            up(place, 1, *load(uin, place, 1))

    row4 = lax.broadcasted_iota(jnp.int32, (4, 128), 0)

    def rows_tile(summed):
        tile = jnp.zeros((4, 128), F32)
        for q in range(4):
            tile = jnp.where(row4 == q, summed[:, 128 * q : 128 * (q + 1)], tile)
        return tile

    def part_copy(e, sender):
        return pltpu.make_async_remote_copy(
            src_ref=gpart.at[e],
            dst_ref=gin.at[sender],
            send_sem=part_send,
            recv_sem=part_recv,
            device_id=at(partner),
            device_id_type=MESH,
        )

    for e in range(2):
        gpart[e] = rows_tile(jnp.sum(gacc[e], axis=0, keepdims=True))

        @pl.when(c != e)
        def _():
            part_copy(e, c).start()

    part_copy(0, 1 - c).wait_recv()
    total = gpart[c] + gin[1 - c]
    gsend[...] = total
    gbox[f] = total

    def g_copy(k):
        return pltpu.make_async_remote_copy(
            src_ref=gsend,
            dst_ref=gbox.at[f],
            send_sem=g_send.at[k],
            recv_sem=g_recv.at[f],
            device_id={"freq": (f + k) % n_freq},
            device_id_type=MESH,
        )

    @pl.loop(1, n_freq)
    def _(k):
        g_copy(k).start()

    @pl.loop(1, n_freq)
    def _(k):
        source = (f + k) % n_freq
        pltpu.make_async_remote_copy(
            src_ref=gsend,
            dst_ref=gbox.at[source],
            send_sem=g_send.at[k],
            recv_sem=g_recv.at[source],
            device_id={"freq": source},
            device_id_type=MESH,
        ).wait_recv()

    total = jnp.sum(gbox[...], axis=0) * (1.0 / (2.0 * n_freq * SHOTS_DEV * n_freq))
    grad_ref[...] = jnp.concatenate([total[q : q + 1] for q in range(4)], axis=1)

    oper_copy(1 - c, c).wait_send()
    par_copy(c).wait_send()
    part_copy(1 - c, c).wait_send()

    @pl.loop(1, n_freq)
    def _(k):
        g_copy(k).wait_send()

    @pl.when(z == 0)
    def _():
        @pl.loop(1, n_freq)
        def _(k):
            box_copy(k).wait_send()

    @pl.loop(0, chunks)
    def _(place):
        @pl.when(z < last)
        def _():
            down_copy(place).wait_send()

        @pl.when(z > 0)
        def _():
            up_copy(place).wait_send()

        tops_here(c, place).wait()
        tops_there(1 - c, place, c).wait_send()
        tops_there(1 - c, place, 1 - c).wait_recv()


def body(traces, shot_of_trace, receiver_cell, slot_freq, operators, slowness, image_model):
    n_freq = lax.axis_size("freq")
    n_depth = lax.axis_size("depth")
    local_freqs = operators.shape[1]
    lateral = operators.shape[-1]
    shot_total = SHOTS_DEV * n_freq
    chunks = shot_total // SH
    block = (2, SH, lateral)
    vmem = pl.BlockSpec(memory_space=pltpu.VMEM)
    dma = pltpu.SemaphoreType.DMA
    gradient, tops = pl.pallas_call(
        functools.partial(kernel, n_depth, n_freq),
        out_shape=(
            jax.ShapeDtypeStruct((1, lateral), F32),
            jax.ShapeDtypeStruct((1, local_freqs, 2, shot_total, lateral), BF16),
        ),
        in_specs=[pl.BlockSpec(memory_space=pltpu.HBM)] * 7,
        out_specs=(vmem, vmem),
        scratch_shapes=[
            pltpu.SMEM(slot_freq.shape, jnp.int32),
            pltpu.VMEM(traces.shape, BF16),
            pltpu.VMEM(shot_of_trace.shape, jnp.int32),
            pltpu.VMEM(receiver_cell.shape, jnp.int32),
            pltpu.VMEM(slowness.shape, F32),
            pltpu.VMEM(image_model.shape, F32),
            pltpu.VMEM((2, 2, lateral, lateral), BF16),
            pltpu.VMEM((2, 2, lateral, lateral), BF16),
            pltpu.VMEM((2, 8, lateral), F32),
            pltpu.VMEM((2, 1, lateral), F32),
            pltpu.VMEM((2, 1, lateral), F32),
            pltpu.VMEM((n_freq, 16, 128), BF16),
            pltpu.VMEM((n_freq, 16, 128), BF16),
            pltpu.VMEM((8, SH + 32, 128), F32),
            pltpu.VMEM((chunks,) + block, BF16),
            pltpu.VMEM((chunks,) + block, BF16),
            pltpu.VMEM((2, chunks) + block, BF16),
            pltpu.VMEM((chunks,) + block, BF16),
            pltpu.VMEM((2, chunks) + block, BF16),
            pltpu.VMEM((2, 8, lateral), F32),
            pltpu.VMEM((2, 4, 128), F32),
            pltpu.VMEM((2, 4, 128), F32),
            pltpu.VMEM((4, 128), F32),
            pltpu.VMEM((n_freq, 4, 128), F32),
            dma((7,)),
            dma(()),
            dma(()),
            dma(()),
            dma(()),
            dma((n_freq,)),
            dma((n_freq,)),
            dma((chunks,)),
            dma((chunks,)),
            dma((chunks,)),
            dma((chunks,)),
            dma((chunks,)),
            dma((chunks,)),
            dma((chunks,)),
            dma(()),
            dma(()),
            dma((n_freq,)),
            dma((n_freq,)),
        ],
        compiler_params=pltpu.CompilerParams(
            collective_id=0, has_side_effects=True, vmem_limit_bytes=48 * 2**20
        ),
        cost_estimate=pl.CostEstimate(flops=2 * 10**9, bytes_accessed=4 * 10**6, transcendentals=4096),
        name="migrate",
    )(
        *[
            pltpu.with_memory_space_constraint(given, pltpu.HBM)
            for given in (slot_freq, traces, shot_of_trace, receiver_cell, slowness, image_model, operators)
        ]
    )
    return gradient, tops


def solution(mesh):
    in_specs = (
        P("freq", None),
        P("freq", None),
        P("freq", None),
        P("freq"),
        P("depth", "freq", None, None, None),
        P("depth", None),
        P("depth", None),
    )
    out_specs = (P("depth", None), P("depth", "freq", None, None, None))
    return jax.shard_map(body, mesh=mesh, in_specs=in_specs, out_specs=out_specs, check_vma=False)
```

time: 91.8 us -> 88.3 us (0.962)
  local copies, waits for them, and re-layouts: 3.32 us -> 1.46 us
  Pallas kernels: 87.7 us -> 86 us
    unnamed x2, local copies, waits for them, and re-layouts: 3.32 us -> 1.46 us
    pallas_call x1, Pallas kernels: 87.7 us -> 86 us  [body(): pl.pallas_call(functools.partial(kernel, n_depth, n_freq), out_shape=(jax...]
where the time goes in v5:
time: 88.3 us; the launch traced here: 88.1 us
  Pallas kernels  86 us (97%)
  local copies, waits for them, and re-layouts  1.46 us (2%)
    pallas_call x1, Pallas kernels, body(): pl.pallas_call(functools.partial(kernel, n_depth, n_freq), out_shape=(jax...  86 us

profile of v5, /device:TPU:1, one launch (start us, length us, event | category | flops | bytes accessed | tf_op | source)
XLA Modules:
  0.0 88.1 jit_solution(5849798265841039430)
XLA Ops:
  0.6 86.0 %migrate.1 = (f32[1,512]{1,0:T(1,128)S(1)}, bf16[1,2,2,192,512]{4,3,2,1,0:T(8,128)(2,1)S(1)}) custom-call(s32[2]{0:T(128)} %slot_hbm.1, bf16[512,128]{1,0:T(8,128)(2,1)} %traces_hbm.1, s32[1,512]{1,0:T(1,128)} %shot_hbm.1, s32[1,512]{1,0:T(1,128)} %cell_hbm.1, f32[1,512]{1,0:T(1,128)} %slow_hbm.1, f32[1,512]{1,0:T(1,128)} %model_hbm.1, ...), custom_call_target="tpu_custom_call" | custom-call | flops 2000000000 | bytes 4000000 | tf_op jit(solution)/shard_map/migrate/pallas_call | solution.py:558
  86.7 0.6 copy.11
  87.3 0.9 copy.12

commit v6 on v5

--- a/solution.py
+++ b/solution.py
@@ -42,6 +42,9 @@
     model_ref,
     opn,
     opt,
+    both_down,
+    both_up,
+    fixed,
     par,
     cosines,
     sines,
@@ -342,20 +345,28 @@
         store(vbuf.at[e], place, n, shifted_real, shifted_imag)
         return jnp.concatenate([shifted_real, shifted_imag], axis=0)
 
-    def forward(e, stacked):
+    def forward(table, stacked):
         rows = stacked.shape[0] // 2
-        by_real, by_imag = product(stacked, opt[e, 0]), product(stacked, opt[e, 1])
+        by_real, by_imag = product(stacked, table[0]), product(stacked, table[1])
         return (by_real[:rows] - by_imag[rows:]).astype(BF16), (by_imag[:rows] + by_real[rows:]).astype(BF16)
 
     def down(place, n, send):
         stacked = shift(0, place, n, *load(din, place, n))
-        real, imag = forward(0, stacked)
+        real, imag = forward(opt.at[0], stacked)
         stacked = shift(1, place, n, real.astype(F32), imag.astype(F32))
         if send:
-            real, imag = forward(1, stacked)
+            real, imag = forward(opt.at[1], stacked)
             store(dout, place, n, real, imag)
             for i in range(n):
                 down_copy(place + i).start()
+
+    def down_inner(place):
+        stacked = shift(0, place, 1, *load(din, place, 1))
+        real, imag = forward(both_down, stacked)
+        store(dout, place, 1, real, imag)
+        down_copy(place).start()
+        real, imag = forward(opt.at[0], stacked)
+        shift(1, place, 1, real.astype(F32), imag.astype(F32))
 
     def rows_of(place):
         return pl.ds(pl.multiple_of(chunk_of(place) * SH, SH), SH)
@@ -373,23 +384,27 @@
             device_id_type=MESH,
         )
 
-    def backward(e, place, n, real, imag):
-        rows = n * SH
+    def back(table, e, real, imag):
+        rows = real.shape[0]
+        stacked = jnp.concatenate([real.astype(BF16), imag.astype(BF16)], axis=0)
+        by_real, by_imag = product(stacked, table[0]), product(stacked, table[1])
+        back_real = by_real[:rows] + by_imag[rows:]
+        back_imag = by_real[rows:] - by_imag[:rows]
+        cos_row, sin_row = cosines[e], sines[e]
+        return cos_row * back_real + sin_row * back_imag, cos_row * back_imag - sin_row * back_real
+
+    def source_of(e, place, n, real, imag):
         old_real, old_imag = load(vbuf.at[e], place, n)
         model = par[e, 1:2, :]
         source_real = real + model * old_real
         source_imag = imag + model * old_imag
         term = old_real * source_real + old_imag * source_imag
-        gacc[e] += jnp.sum(term.reshape(rows // 8, 8, lateral), axis=0)
-        stacked = jnp.concatenate([source_real.astype(BF16), source_imag.astype(BF16)], axis=0)
-        by_real = product(stacked, opn[e, 0])
-        by_imag = product(stacked, opn[e, 1])
-        back_real = by_real[:rows] + by_imag[rows:]
-        back_imag = by_real[rows:] - by_imag[:rows]
-        cos_row, sin_row = cosines[e], sines[e]
-        out_real = (cos_row * back_real + sin_row * back_imag).astype(BF16)
-        out_imag = (cos_row * back_imag - sin_row * back_real).astype(BF16)
-        store(abuf.at[e], place, n, out_real, out_imag)
+        gacc[e] += jnp.sum(term.reshape(n * SH // 8, 8, lateral), axis=0)
+        return source_real, source_imag
+
+    def finish(e, place, n, real, imag):
+        real, imag = real.astype(BF16), imag.astype(BF16)
+        store(abuf.at[e], place, n, real, imag)
         for i in range(n):
             if e == 0:
 
@@ -405,7 +420,22 @@
             def _():
                 tops_there(e, place + i, c).start()
 
-        return out_real.astype(F32), out_imag.astype(F32)
+        return real.astype(F32), imag.astype(F32)
+
+    def backward(e, place, n, real, imag):
+        return finish(e, place, n, *back(opn.at[e], e, *source_of(e, place, n, real, imag)))
+
+    def prepare(place):
+        old_real, old_imag = load(vbuf.at[0], place, 1)
+        model = par[0, 1:2, :]
+        store(fixed, place, 1, *back(opn.at[0], 0, model * old_real, model * old_imag))
+
+    def up_inner(place):
+        real, imag = source_of(1, place, 1, *load(uin, place, 1))
+        fixed_real, fixed_imag = load(fixed, place, 1)
+        top_real, top_imag = back(both_up, 0, real, imag)
+        finish(0, place, 1, top_real + fixed_real, top_imag + fixed_imag)
+        source_of(0, place, 1, *finish(1, place, 1, *back(opn.at[1], 1, real, imag)))
 
     def up(place, n, real, imag):
         real, imag = backward(1, place, n, real, imag)
@@ -428,10 +458,24 @@
 
     @pl.when((z > 0) & (z < last))
     def _():
+        @pl.loop(0, lateral // 64)
+        def _(block):
+            rows = pl.ds(pl.multiple_of(block * 64, 64), 64)
+            real, imag = opt[0, 0, rows, :].astype(F32), opt[0, 1, rows, :].astype(F32)
+            cos_row, sin_row = cosines[1], sines[1]
+            stacked = jnp.concatenate(
+                [(cos_row * real - sin_row * imag).astype(BF16), (cos_row * imag + sin_row * real).astype(BF16)],
+                axis=0,
+            )
+            both_down[0, rows, :], both_down[1, rows, :] = forward(opt.at[1], stacked)
+
+        for p in range(2):
+            both_up[p] = both_down[p].T
+
         @pl.loop(0, chunks)
         def _(place):
             down_copy(place).wait_recv()
-            down(place, 1, True)
+            down_inner(place)
 
     @pl.when(z == last)
     def _():
@@ -450,7 +494,20 @@
         def _(place):
             turn_round(place, 1)
 
-    @pl.when(z < last)
+    inner = (z > 0) & (z < last - 1)
+
+    @pl.when(inner)
+    def _():
+        @pl.loop(0, chunks)
+        def _(place):
+            prepare(place)
+
+        @pl.loop(0, chunks)
+        def _(place):
+            up_copy(place).wait_recv()
+            up_inner(place)
+
+    @pl.when((z == 0) | (z == last - 1))
     def _():
         @pl.loop(0, chunks)
         def _(place):
@@ -572,6 +629,9 @@
             pltpu.VMEM(image_model.shape, F32),
             pltpu.VMEM((2, 2, lateral, lateral), BF16),
             pltpu.VMEM((2, 2, lateral, lateral), BF16),
+            pltpu.VMEM((2, lateral, lateral), BF16),
+            pltpu.VMEM((2, lateral, lateral), BF16),
+            pltpu.VMEM((chunks,) + block, F32),
             pltpu.VMEM((2, 8, lateral), F32),
             pltpu.VMEM((2, 1, lateral), F32),
             pltpu.VMEM((2, 1, lateral), F32),

time: 88.3 us -> 85.8 us (0.972)
  Pallas kernels: 86 us -> 83.5 us
    pallas_call x1, Pallas kernels: 86 us -> 83.5 us  [body(): pl.pallas_call(functools.partial(kernel, n_depth, n_freq), out_shape=(jax...]
where the time goes in v6:
time: 85.8 us; the launch traced here: 85.6 us
  Pallas kernels  83.5 us (97%)
  local copies, waits for them, and re-layouts  1.46 us (2%)
    pallas_call x1, Pallas kernels, body(): pl.pallas_call(functools.partial(kernel, n_depth, n_freq), out_shape=(jax...  83.5 us

profile of v6, /device:TPU:1, one launch (start us, length us, event | category | flops | bytes accessed | tf_op | source)
XLA Modules:
  0.0 85.6 jit_solution(12450398172987429767)
XLA Ops:
  0.6 83.5 %migrate.1 = (f32[1,512]{1,0:T(1,128)S(1)}, bf16[1,2,2,192,512]{4,3,2,1,0:T(8,128)(2,1)S(1)}) custom-call(s32[2]{0:T(128)} %slot_hbm.1, bf16[512,128]{1,0:T(8,128)(2,1)} %traces_hbm.1, s32[1,512]{1,0:T(1,128)} %shot_hbm.1, s32[1,512]{1,0:T(1,128)} %cell_hbm.1, f32[1,512]{1,0:T(1,128)} %slow_hbm.1, f32[1,512]{1,0:T(1,128)} %model_hbm.1, ...), custom_call_target="tpu_custom_call" | custom-call | flops 2000000000 | bytes 4000000 | tf_op jit(solution)/shard_map/migrate/pallas_call | solution.py:615
  84.2 0.6 copy.11
  84.7 0.9 %copy.12 = bf16[1,2,2,192,512]{4,3,2,1,0:T(8,128)(2,1)} copy(bf16[1,2,2,192,512]{4,3,2,1,0:T(8,128)(2,1)S(1)} %get-tuple-element.5) | data formatting | bytes 1572864

commit v7 on v6

--- a/solution.py
+++ b/solution.py
@@ -350,23 +350,25 @@
         by_real, by_imag = product(stacked, table[0]), product(stacked, table[1])
         return (by_real[:rows] - by_imag[rows:]).astype(BF16), (by_imag[:rows] + by_real[rows:]).astype(BF16)
 
-    def down(place, n, send):
+    def down(place, n):
         stacked = shift(0, place, n, *load(din, place, n))
         real, imag = forward(opt.at[0], stacked)
         stacked = shift(1, place, n, real.astype(F32), imag.astype(F32))
-        if send:
-            real, imag = forward(opt.at[1], stacked)
-            store(dout, place, n, real, imag)
-            for i in range(n):
-                down_copy(place + i).start()
-
-    def down_inner(place):
+        real, imag = forward(opt.at[1], stacked)
+        store(dout, place, n, real, imag)
+        for i in range(n):
+            down_copy(place + i).start()
+
+    def down_first(place):
+        down_copy(place).wait_recv()
         stacked = shift(0, place, 1, *load(din, place, 1))
-        real, imag = forward(both_down, stacked)
-        store(dout, place, 1, real, imag)
+        store(dout, place, 1, *forward(both_down, stacked))
         down_copy(place).start()
+
+    def second_step(place, n):
+        stacked = jnp.concatenate([part.astype(BF16) for part in load(vbuf.at[0], place, n)], axis=0)
         real, imag = forward(opt.at[0], stacked)
-        shift(1, place, 1, real.astype(F32), imag.astype(F32))
+        shift(1, place, n, real.astype(F32), imag.astype(F32))
 
     def rows_of(place):
         return pl.ds(pl.multiple_of(chunk_of(place) * SH, SH), SH)
@@ -425,36 +427,85 @@
     def backward(e, place, n, real, imag):
         return finish(e, place, n, *back(opn.at[e], e, *source_of(e, place, n, real, imag)))
 
-    def prepare(place):
-        old_real, old_imag = load(vbuf.at[0], place, 1)
+    def prepare(place, n):
+        old_real, old_imag = load(vbuf.at[0], place, n)
         model = par[0, 1:2, :]
-        store(fixed, place, 1, *back(opn.at[0], 0, model * old_real, model * old_imag))
-
-    def up_inner(place):
+        store(fixed, place, n, *back(opn.at[0], 0, model * old_real, model * old_imag))
+
+    def up_first(place):
+        up_copy(place).wait_recv()
         real, imag = source_of(1, place, 1, *load(uin, place, 1))
+        store(uin, place, 1, real.astype(BF16), imag.astype(BF16))
         fixed_real, fixed_imag = load(fixed, place, 1)
         top_real, top_imag = back(both_up, 0, real, imag)
         finish(0, place, 1, top_real + fixed_real, top_imag + fixed_imag)
-        source_of(0, place, 1, *finish(1, place, 1, *back(opn.at[1], 1, real, imag)))
+
+    def up_rest(place, n):
+        source_of(0, place, n, *finish(1, place, n, *back(opn.at[1], 1, *load(uin, place, n))))
 
     def up(place, n, real, imag):
         real, imag = backward(1, place, n, real, imag)
         backward(0, place, n, real, imag)
 
+    row4 = lax.broadcasted_iota(jnp.int32, (4, 128), 0)
+
+    def rows_tile(summed):
+        tile = jnp.zeros((4, 128), F32)
+        for q in range(4):
+            tile = jnp.where(row4 == q, summed[:, 128 * q : 128 * (q + 1)], tile)
+        return tile
+
+    def part_copy(e, sender):
+        return pltpu.make_async_remote_copy(
+            src_ref=gpart.at[e],
+            dst_ref=gin.at[sender],
+            send_sem=part_send,
+            recv_sem=part_recv,
+            device_id=at(partner),
+            device_id_type=MESH,
+        )
+
+    def g_copy(k):
+        return pltpu.make_async_remote_copy(
+            src_ref=gsend,
+            dst_ref=gbox.at[f],
+            send_sem=g_send.at[k],
+            recv_sem=g_recv.at[f],
+            device_id={"freq": (f + k) % n_freq},
+            device_id_type=MESH,
+        )
+
+    def share_gradient():
+        for e in range(2):
+            gpart[e] = rows_tile(jnp.sum(gacc[e], axis=0, keepdims=True))
+
+            @pl.when(c != e)
+            def _():
+                part_copy(e, c).start()
+
+        part_copy(0, 1 - c).wait_recv()
+        total = gpart[c] + gin[1 - c]
+        gsend[...] = total
+        gbox[f] = total
+
+        @pl.loop(1, n_freq)
+        def _(k):
+            g_copy(k).start()
+
     @pl.when(z == 0)
     def _():
         bin_chunk(0)
-        down(0, 1, True)
+        down(0, 1)
 
         @pl.loop(0, (chunks - 2) // 2)
         def _(turn):
             place = 1 + 2 * turn
             bin_chunk(place)
             bin_chunk(place + 1)
-            down(place, 2, True)
+            down(place, 2)
 
         bin_chunk(chunks - 1)
-        down(chunks - 1, 1, True)
+        down(chunks - 1, 1)
 
     @pl.when((z > 0) & (z < last))
     def _():
@@ -472,91 +523,85 @@
         for p in range(2):
             both_up[p] = both_down[p].T
 
-        @pl.loop(0, chunks)
-        def _(place):
-            down_copy(place).wait_recv()
-            down_inner(place)
+        @pl.loop(0, chunks // 2)
+        def _(turn):
+            down_first(2 * turn)
+            down_first(2 * turn + 1)
+            second_step(2 * turn, 2)
+
+            @pl.when(z == last - 1)
+            def _():
+                prepare(2 * turn, 2)
+
+        @pl.when(z < last - 1)
+        def _():
+            @pl.loop(0, chunks // 2)
+            def _(turn):
+                prepare(2 * turn, 2)
 
     @pl.when(z == last)
     def _():
-        def turn_round(place, n):
+        @pl.loop(0, lateral // 64)
+        def _(block):
+            rows = pl.ds(pl.multiple_of(block * 64, 64), 64)
+            line = lax.broadcasted_iota(jnp.int32, (64, lateral), 0) + block * 64
+            column = lax.broadcasted_iota(jnp.int32, (64, lateral), 1)
+            unit = jnp.where(line == column, 1.0, 0.0).astype(F32)
+            stacked = jnp.concatenate([unit.astype(BF16), jnp.zeros((64, lateral), BF16)], axis=0)
+            real, imag = [part.astype(F32) for part in forward(opt.at[0], stacked)]
+            cos_row, sin_row, model = cosines[1], sines[1], par[1, 1:2, :]
+            real, imag = model * (cos_row * real - sin_row * imag), model * (cos_row * imag + sin_row * real)
+            real, imag = back(opn.at[1], 1, real, imag)
+            real, imag = back(opn.at[0], 0, real + par[0, 1:2, :] * unit, imag)
+            both_down[0, rows, :], both_down[1, rows, :] = real.astype(BF16), imag.astype(BF16)
+
+        def answer(place, n):
             for i in range(n):
                 down_copy(place + i).wait_recv()
-            down(place, n, False)
+            finish(0, place, n, *forward(both_down, shift(0, place, n, *load(din, place, n))))
+
+        def complete(place, n):
+            second_step(place, n)
             nothing = jnp.zeros((n * SH, lateral), F32)
-            up(place, n, nothing, nothing)
+            source = source_of(1, place, n, nothing, nothing)
+            source_of(0, place, n, *finish(1, place, n, *back(opn.at[1], 1, *source)))
 
         @pl.loop(0, (chunks - 2) // 2)
         def _(turn):
-            turn_round(2 * turn, 2)
-
-        @pl.loop(chunks - 2, chunks)
-        def _(place):
-            turn_round(place, 1)
-
-    inner = (z > 0) & (z < last - 1)
-
-    @pl.when(inner)
-    def _():
-        @pl.loop(0, chunks)
-        def _(place):
-            prepare(place)
-
-        @pl.loop(0, chunks)
-        def _(place):
+            answer(2 * turn, 2)
+            complete(2 * turn, 2)
+
+        answer(chunks - 2, 1)
+        answer(chunks - 1, 1)
+        complete(chunks - 2, 2)
+
+    @pl.when((z > 0) & (z < last))
+    def _():
+        @pl.loop(0, chunks // 2)
+        def _(turn):
+            up_first(2 * turn)
+            up_first(2 * turn + 1)
+            up_rest(2 * turn, 2)
+
+    @pl.when(z > 0)
+    def _():
+        share_gradient()
+
+    @pl.when(z == 0)
+    def _():
+        def fetch(place):
             up_copy(place).wait_recv()
-            up_inner(place)
-
-    @pl.when((z == 0) | (z == last - 1))
-    def _():
-        @pl.loop(0, chunks)
-        def _(place):
-            up_copy(place).wait_recv()
-            up(place, 1, *load(uin, place, 1))
-
-    row4 = lax.broadcasted_iota(jnp.int32, (4, 128), 0)
-
-    def rows_tile(summed):
-        tile = jnp.zeros((4, 128), F32)
-        for q in range(4):
-            tile = jnp.where(row4 == q, summed[:, 128 * q : 128 * (q + 1)], tile)
-        return tile
-
-    def part_copy(e, sender):
-        return pltpu.make_async_remote_copy(
-            src_ref=gpart.at[e],
-            dst_ref=gin.at[sender],
-            send_sem=part_send,
-            recv_sem=part_recv,
-            device_id=at(partner),
-            device_id_type=MESH,
-        )
-
-    for e in range(2):
-        gpart[e] = rows_tile(jnp.sum(gacc[e], axis=0, keepdims=True))
-
-        @pl.when(c != e)
-        def _():
-            part_copy(e, c).start()
-
-    part_copy(0, 1 - c).wait_recv()
-    total = gpart[c] + gin[1 - c]
-    gsend[...] = total
-    gbox[f] = total
-
-    def g_copy(k):
-        return pltpu.make_async_remote_copy(
-            src_ref=gsend,
-            dst_ref=gbox.at[f],
-            send_sem=g_send.at[k],
-            recv_sem=g_recv.at[f],
-            device_id={"freq": (f + k) % n_freq},
-            device_id_type=MESH,
-        )
-
-    @pl.loop(1, n_freq)
-    def _(k):
-        g_copy(k).start()
+            up_copy(place + 1).wait_recv()
+            return load(uin, place, 2)
+
+        @pl.loop(0, chunks // 2 - 1)
+        def _(turn):
+            up(2 * turn, 2, *fetch(2 * turn))
+
+        place = chunks - 2
+        source = source_of(0, place, 2, *backward(1, place, 2, *fetch(place)))
+        share_gradient()
+        finish(0, place, 2, *back(opn.at[0], 0, *source))
 
     @pl.loop(1, n_freq)
     def _(k):

time: 85.8 us -> 83.8 us (0.977)
  Pallas kernels: 83.5 us -> 81.6 us
    pallas_call x1, Pallas kernels: 83.5 us -> 81.6 us  [body(): pl.pallas_call(functools.partial(kernel, n_depth, n_freq), out_shape=(jax...]
where the time goes in v7:
time: 83.8 us; the launch traced here: 83.7 us
  Pallas kernels  81.6 us (97%)
  local copies, waits for them, and re-layouts  1.46 us (2%)
    pallas_call x1, Pallas kernels, body(): pl.pallas_call(functools.partial(kernel, n_depth, n_freq), out_shape=(jax...  81.6 us

profile of v7, /device:TPU:1, one launch (start us, length us, event | category | flops | bytes accessed | tf_op | source)
XLA Modules:
  0.0 83.7 jit_solution(14051003790231230129)
XLA Ops:
  0.6 81.6 %migrate.1 = (f32[1,512]{1,0:T(1,128)S(1)}, bf16[1,2,2,192,512]{4,3,2,1,0:T(8,128)(2,1)S(1)}) custom-call(s32[2]{0:T(128)} %slot_hbm.1, bf16[512,128]{1,0:T(8,128)(2,1)} %traces_hbm.1, s32[1,512]{1,0:T(1,128)} %shot_hbm.1, s32[1,512]{1,0:T(1,128)} %cell_hbm.1, f32[1,512]{1,0:T(1,128)} %slow_hbm.1, f32[1,512]{1,0:T(1,128)} %model_hbm.1, ...), custom_call_target="tpu_custom_call" | custom-call | flops 2000000000 | bytes 4000000 | tf_op jit(solution)/shard_map/migrate/pallas_call | solution.py:660
  82.2 0.6 copy.11
  82.8 0.9 %copy.12 = bf16[1,2,2,192,512]{4,3,2,1,0:T(8,128)(2,1)} copy(bf16[1,2,2,192,512]{4,3,2,1,0:T(8,128)(2,1)S(1)} %get-tuple-element.5) | data formatting | bytes 1572864

commit v8 on v7

--- a/solution.py
+++ b/solution.py
@@ -568,7 +568,8 @@
 
         @pl.loop(0, (chunks - 2) // 2)
         def _(turn):
-            answer(2 * turn, 2)
+            answer(2 * turn, 1)
+            answer(2 * turn + 1, 1)
             complete(2 * turn, 2)
 
         answer(chunks - 2, 1)

time: 83.8 us -> 83.7 us (level)
  no operation moved by 1% of the time
where the time goes in v8:
time: 83.7 us; the launch traced here: 83.6 us
  Pallas kernels  81.5 us (97%)
  local copies, waits for them, and re-layouts  1.46 us (2%)
    pallas_call x1, Pallas kernels, body(): pl.pallas_call(functools.partial(kernel, n_depth, n_freq), out_shape=(jax...  81.5 us

profile of v8, /device:TPU:1, one launch (start us, length us, event | category | flops | bytes accessed | tf_op | source)
XLA Modules:
  0.0 83.6 jit_solution(4197348750533624787)
XLA Ops:
  0.6 81.5 %migrate.1 = (f32[1,512]{1,0:T(1,128)S(1)}, bf16[1,2,2,192,512]{4,3,2,1,0:T(8,128)(2,1)S(1)}) custom-call(s32[2]{0:T(128)} %slot_hbm.1, bf16[512,128]{1,0:T(8,128)(2,1)} %traces_hbm.1, s32[1,512]{1,0:T(1,128)} %shot_hbm.1, s32[1,512]{1,0:T(1,128)} %cell_hbm.1, f32[1,512]{1,0:T(1,128)} %slow_hbm.1, f32[1,512]{1,0:T(1,128)} %model_hbm.1, ...), custom_call_target="tpu_custom_call" | custom-call | flops 2000000000 | bytes 4000000 | tf_op jit(solution)/shard_map/migrate/pallas_call | solution.py:661
  82.1 0.6 copy.11
  82.7 0.9 %copy.12 = bf16[1,2,2,192,512]{4,3,2,1,0:T(8,128)(2,1)} copy(bf16[1,2,2,192,512]{4,3,2,1,0:T(8,128)(2,1)S(1)} %get-tuple-element.5) | data formatting | bytes 1572864
